TPU v7x, 512 devices: a whole 4x8x8 slice. The times are simulated.
512 devices in a mesh: probe: 4 (over x), sky: 128 (over y, z, core).
Axes of the slice: x: 4, y: 8, z: 8, core: 2. Of those that a mesh axis runs over, the one named last changes fastest.
Arguments:
- legendre: float32 [256, 4096, 512], P('sky', 'probe'), may hold values from -2.6958446 to 2.6958446
- signs: int32 [4, 512, 8192], P('probe', 'sky'), may hold values from -1 to 1, as said below
- inv_noise: float32 [512, 8192], P('sky'), may hold values from 0.3 to 3
- inv_signal: float32 [4096], replicated, may hold values from 0.3 to 30
- harmonic_order_values: int32 [256], replicated, may hold values from 0 to 4095, as said below
- cycle_rows: int32 [512], replicated, may hold values from 0 to 511, each once
Outputs:
- residual: float32 [4, 256, 2, 4096], P('probe', 'sky')
- variance: float32 [512, 8192], P('sky')
Inputs may be any that keep to these rules, and one draw needn't show every extreme that they name: `harmonic_order_values`: slots 2i and 2i + 1 hold an order m and 4095 - m; no order appears twice; order 0 appears. `signs`: every entry is -1 or 1.
All inputs are finite; a program needn't handle non-finite values.
Results may differ from a plain program's by a relative error of at most 0.0003.
Values sent between devices are 32-bit elements; how exact they have to be, the bound alone decides.
No kernel may reach another device: no remote copies, remote signals or barrier semaphores. Data moves between devices by JAX's collectives and lax.ppermute only.
A program may use at most 64 MiB of HBM per device.

v0:
```python
import math

import jax
import jax.numpy as jnp
from jax import lax
from jax.sharding import PartitionSpec as P

MULTIPOLE_LIMIT = lax.Precision.HIGHEST


def phase_tables(orders, cycle_length):
    inner_width = 128
    outer_width = cycle_length // inner_width
    outer_steps = jnp.arange(outer_width)
    inner_steps = jnp.arange(inner_width)
    outer_angles = (orders[:, None] * outer_steps[None, :] % outer_width).astype(jnp.float32) * (
        2.0 * math.pi / outer_width
    )
    inner_angles = (orders[:, None] * inner_steps[None, :] % cycle_length).astype(jnp.float32) * (
        2.0 * math.pi / cycle_length
    )
    scale_factor = 1.0 / math.sqrt(cycle_length)
    return (
        jnp.cos(outer_angles),
        jnp.sin(outer_angles),
        jnp.cos(inner_angles) * scale_factor,
        jnp.sin(inner_angles) * scale_factor,
    )


def cycle_analysis(pixels, tables, cycle_rows):
    outer_cosine, outer_sine, inner_cos, inner_sin = tables
    cycle_count = pixels.shape[0]
    folded_result = pixels.reshape(cycle_count, outer_cosine.shape[1], inner_cos.shape[1])
    real_component = jnp.einsum(
        "eq,fqj->efj", outer_cosine, folded_result, precision=MULTIPOLE_LIMIT
    )
    imaginary_component = jnp.einsum(
        "eq,fqj->efj", outer_sine, folded_result, precision=MULTIPOLE_LIMIT
    )
    cos_terms = jnp.sum(
        inner_cos[:, None, :] * real_component - inner_sin[:, None, :] * imaginary_component, axis=2
    )
    sin_terms = jnp.sum(
        inner_sin[:, None, :] * real_component + inner_cos[:, None, :] * imaginary_component, axis=2
    )
    harmonic_coefficient_set = jnp.stack([cos_terms, sin_terms], axis=1)
    local_orders = lax.all_to_all(
        harmonic_coefficient_set, "sky", split_axis=0, concat_axis=2, tiled=True
    )
    return jnp.zeros_like(local_orders).at[:, :, cycle_rows].set(local_orders)


def degree_terms(masked_sky_map, latitude):
    return jnp.einsum(
        "klr,pkcr->pkcl",
        masked_sky_map,
        lax.all_gather(latitude[None], "probe", axis=0, tiled=True),
        precision=MULTIPOLE_LIMIT,
    )


def synthesize(split_coeffs, masked_sky_map, tables, cycle_rows, cycle_length):
    outer_cosine, outer_sine, inner_cos, inner_sin = tables
    probe_fields = lax.psum_scatter(
        jnp.einsum("klr,pkcl->pkcr", masked_sky_map, split_coeffs, precision=MULTIPOLE_LIMIT),
        "probe",
        scatter_dimension=0,
        tiled=True,
    )
    slot_order = jnp.take(probe_fields[0], cycle_rows, axis=2)
    by_cycle = lax.all_to_all(slot_order, "sky", split_axis=2, concat_axis=0, tiled=True)
    cos_coeffs = by_cycle[:, 0, :][:, :, None]
    sin_coeffs = by_cycle[:, 1, :][:, :, None]
    rotated_real = cos_coeffs * inner_cos[:, None, :] + sin_coeffs * inner_sin[:, None, :]
    rotated_imaginary = cos_coeffs * inner_sin[:, None, :] - sin_coeffs * inner_cos[:, None, :]
    folded_result = jnp.einsum("fon,fz->ozn", rotated_real, outer_cosine, precision=MULTIPOLE_LIMIT)
    folded_result = folded_result - jnp.einsum(
        "fon,fz->ozn", rotated_imaginary, outer_sine, precision=MULTIPOLE_LIMIT
    )
    return folded_result.reshape(by_cycle.shape[2], cycle_length)


def join_degrees(split_coeffs):
    return lax.all_to_all(split_coeffs, "probe", split_axis=0, concat_axis=3, tiled=True)


def total_norm_value(local_terms):
    return lax.psum(local_terms, ("probe", "sky"))


def curve_total(local_terms):
    return lax.psum(local_terms, ("probe", "sky"))


def per_device(legendre, signs, inv_noise, inv_signal, harmonic_order_values, cycle_rows):
    slots_per_worker = legendre.shape[0]
    quarter = legendre.shape[1]
    cycle_length = signs.shape[2]
    probe_count = lax.axis_size("probe")
    probe_place = lax.axis_index("probe")
    sky_place = lax.axis_index("sky")
    own_probe = jnp.arange(probe_count, dtype=jnp.int32) == probe_place
    my_orders = lax.dynamic_slice_in_dim(
        harmonic_order_values, sky_place * slots_per_worker, slots_per_worker
    )
    degrees = probe_place * quarter + jnp.arange(quarter, dtype=jnp.int32)
    masked_sky_map = jnp.where((degrees[None, :] >= my_orders[:, None])[:, :, None], legendre, 0.0)
    tables = phase_tables(harmonic_order_values, cycle_length)
    sign_field = signs[0].astype(jnp.float32)
    first_split = degree_terms(masked_sky_map, cycle_analysis(sign_field, tables, cycle_rows))
    first_terms = join_degrees(first_split)
    norm_local = jnp.where(own_probe, jnp.sum(first_terms * first_terms), 0.0)
    norm_all = total_norm_value(norm_local)
    mapped = synthesize(first_split, masked_sky_map, tables, cycle_rows, cycle_length)
    weighted = sign_field * mapped
    noise_split = degree_terms(
        masked_sky_map, cycle_analysis(inv_noise * mapped, tables, cycle_rows)
    )
    image_terms = inv_signal[None, None, None, :] * first_terms + join_degrees(noise_split)
    curve_local = jnp.where(own_probe, jnp.sum(first_terms * image_terms), 0.0)
    curve_all = curve_total(curve_local)
    step_ratio = norm_all / curve_all
    own_ratio = jnp.sum(jnp.where(own_probe, step_ratio, 0.0))
    residual = first_terms - own_ratio * image_terms
    variance = lax.psum(own_ratio * weighted, "probe") / probe_count
    return (residual, variance)


def solution(mesh):
    in_specs = (P("sky", "probe", None), P("probe", "sky", None), P("sky", None), P(), P(), P())
    out_specs = (P("probe", "sky", None, None), P("sky", None))
    return jax.shard_map(
        per_device, mesh=mesh, in_specs=in_specs, out_specs=out_specs, check_vma=False
    )
```

profile of v0, /device:TPU:1, one launch (start us, length us, event | category | flops | bytes accessed | tf_op | source)
XLA Modules:
  0.0 353.3 jit_solution(8436593122437280639)
XLA Ops:
  7.2 1.2 cosine_multiply_fusion
  8.4 0.9 convert_bitcast_fusion
  9.3 1.5 fusion.51
  10.8 1.6 subtract_reduce_fusion.1
  13.3 18.4 %all-to-all-start = ((f32[256,2,4]{2,1,0:T(2,128)}), f32[256,2,4]{2,1,0:T(2,128)S(1)}, u32[]{:S(2)}, u32[]{:S(2)}) async-start(f32[256,2,4]{2,1,0:T(2,128)} %copy.59), calls=%async_computation | async-start | bytes 524288 | tf_op jit(solution)/shard_map/all_to_all | solution.py:48
  34.0 1.3 dynamic-slice
  35.3 10.7 %all-to-all-done = f32[256,2,4]{2,1,0:T(2,128)S(1)} async-done(((f32[256,2,4]{2,1,0:T(2,128)}), f32[256,2,4]{2,1,0:T(2,128)S(1)}, u32[]{:S(2)}, u32[]{:S(2)}) %all-to-all-start) | async-done | bytes 8224 | tf_op jit(solution)/shard_map/all_to_all | solution.py:48
  46.6 13.6 %scatter_fusion = f32[2,2,512]{1,0,2:T(2,128)S(1)} fusion(f32[2,2,512]{1,0,2:T(2,128)S(1)} %broadcast.135.clone, s32[512]{0:T(512)S(1)} %compare_select_fusion, f32[512,2,2]{2,1,0:T(2,128)S(1)} %copy.62), kind=kCustom, calls=%fused_computation.1 | custom fusion | bytes 26624 | tf_op jit(solution)/shard_map/scatter | solution.py:51
  60.4 9.5 %all-gather = f32[8,2,512]{2,1,0:T(2,128)S(1)} all-gather(f32[2,2,512]{2,1,0:T(2,128)S(1)} %copy.63), channel_id=2, replica_groups=mesh['probe'=4,'sky'=128] {'probe'}, dimensions={0}, use_global_device_ids=true | all-gather | bytes 40960 | tf_op jit(solution)/shard_map/all_gather | solution.py:58
  69.9 5.8 %fusion.16 = f32[4,2,2,1024]{3,0,2,1:T(4,128)S(1)} fusion(f32[2,1024,512]{2,1,0:T(8,128)} %param.6, pred[2,1024]{1,0:T(4,128)(4,1)S(1)} %broadcast_compare_fusion, f32[4,2,2,512]{3,2,1,0:T(2,128)S(1)} %bitcast.137), kind=kOutput, calls=%fused_computation.20 | convolution fusion | flops 101711872 | bytes 4294656 | tf_op jit(solution)/shard_map/klr,pkcr->pkcl/dot_general | solution.py:55
  75.7 2.7 fusion.22
  78.4 13.4 %all-reduce = f32[4,2,2,512]{3,2,1,0:T(2,128)S(1)} all-reduce(f32[4,2,2,512]{3,2,1,0:T(2,128)S(1)} %copy.67), channel_id=4, replica_groups=mesh['probe'=4,'sky'=128] {'probe'}, use_global_device_ids=true, to_apply=%region_5.6.clone | all-reduce | flops 8192 | bytes 65536
  92.7 2.1 gather_fusion
  94.8 1.8 select_bitcast_fusion
  96.6 32.4 %all_to_all.90 = f32[2,2,512]{1,0,2:T(2,128)S(1)} all-to-all(f32[2,2,512]{1,0,2:T(2,128)S(1)} %select_bitcast_fusion), channel_id=1, replica_groups=mesh['probe'=4,'sky'=128] {'sky'}, dimensions={2} | all-to-all | bytes 16384 | tf_op jit(solution)/shard_map/all_to_all | solution.py:72
  129.0 1.7 copy.86
  131.2 0.9 fusion.28
  133.9 1.0 subtract_reduce_fusion
  135.8 7.3 %all-to-all-start.3 = ((f32[256,2,4]{2,1,0:T(2,128)}), f32[256,2,4]{2,1,0:T(2,128)S(1)}, u32[]{:S(2)}, u32[]{:S(2)}) async-start(f32[256,2,4]{2,1,0:T(2,128)} %copy.75), calls=%async_computation.3 | async-start | bytes 524288 | tf_op jit(solution)/shard_map/all_to_all | solution.py:48
  143.7 13.7 %all-to-all-done.3 = f32[256,2,4]{2,1,0:T(2,128)S(1)} async-done(((f32[256,2,4]{2,1,0:T(2,128)}), f32[256,2,4]{2,1,0:T(2,128)S(1)}, u32[]{:S(2)}, u32[]{:S(2)}) %all-to-all-start.3) | async-done | bytes 8224 | tf_op jit(solution)/shard_map/all_to_all | solution.py:48
  157.4 3.3 all-to-all-start.1
  161.3 13.6 %scatter_fusion.1 = f32[2,2,512]{1,0,2:T(2,128)S(1)} fusion(f32[2,2,512]{1,0,2:T(2,128)S(1)} %broadcast.135, s32[512]{0:T(512)S(1)} %compare_select_fusion, f32[512,2,2]{2,1,0:T(2,128)S(1)} %copy.78), kind=kCustom, calls=%fused_computation.2 | custom fusion | bytes 26624 | tf_op jit(solution)/shard_map/scatter | solution.py:51
  175.1 9.6 %all-gather.1 = f32[8,2,512]{2,1,0:T(2,128)S(1)} all-gather(f32[2,2,512]{2,1,0:T(2,128)S(1)} %copy.79), channel_id=3, replica_groups=mesh['probe'=4,'sky'=128] {'probe'}, dimensions={0}, use_global_device_ids=true | all-gather | bytes 40960 | tf_op jit(solution)/shard_map/all_gather | solution.py:58
  184.6 5.8 %fusion.19 = f32[4,2,2,1024]{3,0,2,1:T(4,128)S(1)} fusion(f32[2,1024,512]{2,1,0:T(8,128)} %param.6, pred[2,1024]{1,0:T(4,128)(4,1)S(1)} %broadcast_compare_fusion, f32[4,2,2,512]{3,2,1,0:T(2,128)S(1)} %bitcast.136), kind=kOutput, calls=%fused_computation.21 | convolution fusion | flops 101711872 | bytes 4294656 | tf_op jit(solution)/shard_map/klr,pkcr->pkcl/dot_general | solution.py:55
  191.1 3.4 all-to-all-start.4
  194.5 4.4 %all-to-all-done.4 = f32[4,2,2,1024]{3,2,1,0:T(2,128)S(1)} async-done(((f32[4,2,2,1024]{3,2,1,0:T(2,128)}), f32[4,2,2,1024]{3,2,1,0:T(2,128)S(1)}, u32[]{:S(2)}, u32[]{:S(2)}) %all-to-all-start.4) | async-done | bytes 65568 | tf_op jit(solution)/shard_map/all_to_all | solution.py:85
  199.6 1.3 fusion.85
  200.9 98.7 %all-reduce.1 = (f32[4]{0:T(128)S(1)}, f32[4]{0:T(128)S(1)}) all-reduce(f32[4]{0:T(128)S(1)} %get-tuple-element.15, f32[4]{0:T(128)S(1)} %get-tuple-element.14), channel_id=1, replica_groups=mesh['probe'=4,'sky'=128] {'probe','sky'}, use_global_device_ids=true, to_apply=%region_4.5 | all-reduce | flops 8 | bytes 64 | tf_op jit(solution)/shard_map/psum | solution.py:89
  300.3 1.3 fusion.48
  301.6 1.2 multiply_subtract_fusion
  302.8 42.0 %all-reduce.4.cloned.1.call-done = f32[4,8192]{1,0:T(4,128)} async-done(((f32[4,8192]{1,0:T(4,128)}), f32[4,8192]{1,0:T(4,128)}) %all-reduce.4.cloned.1.call-update) | async-done | bytes 131088 | tf_op jit(solution)/shard_map/psum | solution.py:126
  344.9 1.6 broadcast_multiply_fusion
  (52 shorter events, 11.4 us)
Async XLA Ops:
  13.3 32.6 %all-to-all-start = ((f32[256,2,4]{2,1,0:T(2,128)}), f32[256,2,4]{2,1,0:T(2,128)S(1)}, u32[]{:S(2)}, u32[]{:S(2)}) async-start(f32[256,2,4]{2,1,0:T(2,128)} %copy.59), calls=%async_computation | async-start | bytes 524288 | tf_op jit(solution)/shard_map/all_to_all | solution.py:48
  60.4 15.3 %copy-start = (f32[2,1024,512]{2,1,0:T(8,128)S(1)}, f32[2,1024,512]{2,1,0:T(8,128)}, u32[]{:S(2)}) copy-start(f32[2,1024,512]{2,1,0:T(8,128)} %param.6) | copy-start | bytes 12582916
  75.7 55.5 %copy-start.4 = (s32[256]{0:T(256)S(1)}, s32[256]{0:T(256)}, u32[]{:S(2)}) copy-start(s32[256]{0:T(256)} %param.10) | copy-start | bytes 3076
  78.4 54.6 %copy-start.2 = (f32[4,8192]{1,0:T(4,128)S(1)}, f32[4,8192]{1,0:T(4,128)}, u32[]{:S(2)}) copy-start(f32[4,8192]{1,0:T(4,128)} %param.8) | copy-start | bytes 393220
  135.7 58.7 %copy-start.3 = (f32[4096]{0:T(1024)S(1)}, f32[4096]{0:T(1024)}, u32[]{:S(2)}) copy-start(f32[4096]{0:T(1024)} %param.9) | copy-start | bytes 49156
  135.8 21.6 %all-to-all-start.3 = ((f32[256,2,4]{2,1,0:T(2,128)}), f32[256,2,4]{2,1,0:T(2,128)S(1)}, u32[]{:S(2)}, u32[]{:S(2)}) async-start(f32[256,2,4]{2,1,0:T(2,128)} %copy.75), calls=%async_computation.3 | async-start | bytes 524288 | tf_op jit(solution)/shard_map/all_to_all | solution.py:48
  143.0 157.2 %copy-start.1 = (s32[1,4,8192]{2,1,0:T(4,128)S(1)}, s32[1,4,8192]{2,1,0:T(4,128)}, u32[]{:S(2)}) copy-start(s32[1,4,8192]{2,1,0:T(4,128)} %param.7) | copy-start | bytes 393220
  157.4 33.7 %all-to-all-start.1 = ((f32[4,2,2,1024]{3,2,1,0:T(2,128)}), f32[4,2,2,1024]{3,2,1,0:T(2,128)S(1)}, u32[]{:S(2)}, u32[]{:S(2)}) async-start(f32[4,2,2,1024]{3,2,1,0:T(2,128)} %copy.65), calls=%async_computation.1 | async-start | bytes 131072 | tf_op jit(solution)/shard_map/all_to_all | solution.py:85
  191.1 7.8 %all-to-all-start.4 = ((f32[4,2,2,1024]{3,2,1,0:T(2,128)}), f32[4,2,2,1024]{3,2,1,0:T(2,128)S(1)}, u32[]{:S(2)}, u32[]{:S(2)}) async-start(f32[4,2,2,1024]{3,2,1,0:T(2,128)} %copy.81), calls=%async_computation.4 | async-start | bytes 131072 | tf_op jit(solution)/shard_map/all_to_all | solution.py:85
  194.4 150.4 %all-reduce.4.cloned.1.call-start = ((), (), s32[]{:S(2)}) async-start(), calls=%async_computation.5 | async-start | bytes 262144 | tf_op jit(solution)/shard_map/psum | solution.py:126
Sparse Core Ops, SparseCore 0:
  301.7 43.0 all-reduce.3
where the time goes:
time: 355 us; the launch traced here: 353 us
  blocking collectives  164 us (46%)
  waiting for transfers between devices  70.9 us (20%)
  local copies, waits for them, and re-layouts  39 us (11%)
  starting transfers between devices  32.3 us (9%)
  matrix products  21 us (6%)
  between operations  14.3 us (4%)
  other arithmetic  12.2 us (3%)
    psum x1, blocking collectives, total_norm_value(): return lax.psum(local_terms, ('probe', 'sky'))  98.7 us
    psum x1, waiting for transfers between devices, per_device(): variance = lax.psum(own_ratio * weighted, 'probe') / probe_count  42 us
    all_to_all x1, blocking collectives, synthesize(): lax.all_to_all(slot_order, 'sky', split_axis=2, concat_axis=0, tiled=True)  32.4 us
    scatter x4, local copies, waits for them, and re-layouts, cycle_analysis(): return jnp.zeros_like(local_orders).at[:, :, cycle_rows].set(local_orders)  27.5 us
    all_to_all x2, starting transfers between devices, cycle_analysis(): lax.all_to_all(harmonic_coefficient_set, 'sky', split_axis=0, concat_axis...  25.7 us
    all_to_all x2, waiting for transfers between devices, cycle_analysis(): lax.all_to_all(harmonic_coefficient_set, 'sky', split_axis=0, concat_axis...  24.4 us
    all_gather x2, blocking collectives, degree_terms(): lax.all_gather(latitude[None], 'probe', axis=0, tiled=True)  19.1 us
    unnamed x1, blocking collectives  13.4 us
  transfers between devices with their start and end apart: 5, of which 4 were waited for; matrix products, arithmetic and copies ran while one was open for 7% of the time, Pallas kernels for 0%

commit v1 on v0

v1 whole, which is shorter than its diff:
```python
import functools
import math

import jax
import jax.numpy as jnp
from jax import lax
from jax.experimental import pallas as pl
from jax.experimental.pallas import tpu as pltpu
from jax.sharding import PartitionSpec as P

F32 = jnp.float32
BF16 = jnp.bfloat16
LANES = 128
SCALARS = 64
VMEM_BYTES = 40 * 1024 * 1024


def iota(shape, dim):
    return lax.broadcasted_iota(jnp.int32, shape, dim)


def dot(a, b):
    return jnp.dot(a, b, preferred_element_type=F32)


def halves(value):
    high = value.astype(BF16)
    return high, (value - high.astype(F32)).astype(BF16)


def turn(value, lanes):
    lanes = lanes % LANES
    return pltpu.roll(value, lanes, 1) if lanes else value


def fold(flat_ref, folded_ref):
    cycles = flat_ref.shape[-2]
    for j in range(folded_ref.shape[0] // cycles):
        folded_ref[j * cycles : (j + 1) * cycles, :] = flat_ref[
            :, j * LANES : (j + 1) * LANES
        ].astype(F32)


def twiddle_sums(parts, inner_cos, inner_sin, acc, lane, base):
    count = inner_cos.shape[0]
    real, imag = parts[:count], parts[count:]
    cos_sum = jnp.sum(inner_cos * real - inner_sin * imag, axis=1, keepdims=True)
    sin_sum = jnp.sum(inner_sin * real + inner_cos * imag, axis=1, keepdims=True)
    acc = jnp.where(lane == base, cos_sum, acc)
    return jnp.where(lane == base + 1, sin_sum, acc)


def join_slots(by_order_ref, slots, width):
    places = by_order_ref.shape[0] // slots
    out = by_order_ref[pl.ds(0, places, stride=slots), :]
    for s in range(1, slots):
        out = out + turn(by_order_ref[pl.ds(s, places, stride=slots), :], s * width)
    return out


def first_kernel(
    slots, orders_ref, signs_ref, send_ref, inner_cos_ref, inner_sin_ref, outer_a_ref, outer_s_ref,
    folded_ref, sums_ref,
):
    count = orders_ref.shape[1]
    probes = send_ref.shape[0]
    cycles = signs_ref.shape[1]
    outer = folded_ref.shape[0] // cycles
    cycle_length = outer * LANES
    own = lax.axis_index("probe")

    order_row = orders_ref[...]
    order_col = jnp.sum(
        jnp.where(iota((count, count), 0) == iota((count, count), 1), order_row.astype(F32), 0.0),
        axis=1,
        keepdims=True,
    ).astype(jnp.int32)
    inner_angles = ((order_col * iota((count, LANES), 1)) & (cycle_length - 1)).astype(F32) * (
        2.0 * math.pi / cycle_length
    )
    scale_factor = 1.0 / math.sqrt(cycle_length)
    inner_cos = jnp.cos(inner_angles) * scale_factor
    inner_sin = jnp.sin(inner_angles) * scale_factor
    inner_cos_ref[...] = inner_cos
    inner_sin_ref[...] = inner_sin
    step = 2.0 * math.pi / outer
    twice = ((order_col * iota((count, LANES), 1)) & (outer - 1)).astype(F32) * step
    cos_hi, cos_lo = halves(jnp.cos(twice))
    sin_hi, sin_lo = halves(jnp.sin(twice))
    outer_a_ref[:count, :LANES] = cos_hi
    outer_a_ref[:count, LANES:] = cos_lo
    outer_a_ref[count:, :LANES] = sin_hi
    outer_a_ref[count:, LANES:] = sin_lo
    across = ((order_row * iota((outer, count), 0)) & (outer - 1)).astype(F32) * step
    cos_hi, cos_lo = halves(jnp.cos(across))
    sin_hi, sin_lo = halves(-jnp.sin(across))
    outer_s_ref[:outer, :count] = cos_hi
    outer_s_ref[:outer, count:] = sin_hi
    outer_s_ref[outer:, :count] = cos_lo
    outer_s_ref[outer:, count:] = sin_lo

    fold(signs_ref.at[0], folded_ref)
    pixels = jnp.concatenate(
        [folded_ref[pl.ds(f, outer, stride=cycles), :] for f in range(cycles)], axis=1
    ).astype(BF16)
    parts = dot(outer_a_ref[:, :outer], pixels) + dot(
        outer_a_ref[:, LANES : LANES + outer], pixels
    )
    lane = iota((count, LANES), 1)
    acc = jnp.zeros((count, LANES), F32)
    width = slots * probes * 2
    for f in range(cycles):
        acc = twiddle_sums(
            parts[:, f * LANES : (f + 1) * LANES], inner_cos, inner_sin, acc, lane,
            f * width + own * 2,
        )
    sums_ref[...] = acc
    out = join_slots(sums_ref, slots, probes * 2)
    for p in range(probes):
        send_ref[p] = out


def latitude_columns(received, rows_ref, slots, probes, stack_ref):
    places = received.shape[0]
    total = rows_ref.shape[1]
    cycles = total // places
    width = slots * probes * 2
    lane = iota((places, LANES), 1)
    for f in range(cycles):
        value = turn(received, -f * width)
        high = value.astype(BF16).astype(F32)
        low = turn(value - high, width)
        stack_ref[pl.ds(f, places, stride=cycles), :] = jnp.where(
            lane < width, high, jnp.where(lane < 2 * width, low, 0.0)
        )
    chosen = jnp.where(iota((total, total), 0) == rows_ref[...], 1.0, 0.0).astype(BF16)
    return dot(chosen, stack_ref[...].astype(BF16)).astype(BF16), chosen


def degree_sums(leg_hi, leg_lo, columns, k, slots, probes, order, first_degree):
    rows = probes * 2
    width = slots * rows
    across = (dot(leg_hi, columns) + dot(leg_lo, columns)).T
    terms = across[k * rows : (k + 1) * rows] + across[
        width + k * rows : width + (k + 1) * rows
    ]
    degrees = first_degree + iota(terms.shape, 1)
    return jnp.where(degrees >= order, terms, 0.0)


def second_kernel(
    slots, orders_ref, received_ref, rows_ref, inv_signal_ref, legendre_ref,
    send_ref, terms_ref, stack_ref, spread_ref,
):
    probes = send_ref.shape[0]
    places = send_ref.shape[1]
    quarter = legendre_ref.shape[1]
    total = rows_ref.shape[1]
    cycles = total // places
    rows = probes * 2
    width = slots * rows
    own = lax.axis_index("probe")
    first_slot = lax.axis_index("sky") * slots

    received = received_ref[:places]
    for p in range(1, probes):
        received = received + received_ref[p * places : (p + 1) * places]
    columns, chosen = latitude_columns(received, rows_ref, slots, probes, stack_ref)
    first_degree = own * quarter
    signal = inv_signal_ref[:, pl.ds(pl.multiple_of(first_degree, LANES), quarter)]
    norm = jnp.zeros((rows, 1), F32)
    prior = jnp.zeros((rows, 1), F32)
    fields = []
    for k in range(slots):
        leg_hi, leg_lo = halves(legendre_ref[k])
        terms = degree_sums(
            leg_hi, leg_lo, columns, k, slots, probes, orders_ref[first_slot + k], first_degree
        )
        terms_ref[k] = terms
        squares = terms * terms
        norm = norm + jnp.sum(squares, axis=1, keepdims=True)
        prior = prior + jnp.sum(squares * signal, axis=1, keepdims=True)
        both = jnp.concatenate(halves(terms), axis=0)
        field = dot(both, leg_hi) + dot(both, leg_lo)
        fields.append(field[:rows] + field[rows:])
    fields = jnp.concatenate(fields, axis=0)
    both = jnp.concatenate(halves(fields), axis=0)
    by_cycle = dot(both, chosen)
    by_cycle = by_cycle[:width] + by_cycle[width:]
    spread_ref[...] = jnp.concatenate(
        [by_cycle, jnp.zeros((LANES - width, total), F32)], axis=0
    ).T
    row, lane = iota((rows, LANES), 0), iota((rows, LANES), 1)
    scalars = jnp.where(lane == SCALARS + row // 2, norm, 0.0)
    scalars = scalars + jnp.where(lane == SCALARS + probes + row // 2, prior, 0.0)
    out = jnp.broadcast_to(jnp.sum(scalars, axis=0, keepdims=True), (places, LANES))
    for f in range(cycles):
        out = out + turn(spread_ref[pl.ds(f, places, stride=cycles), :], f * width)
    for p in range(probes):
        send_ref[p] = out


def third_kernel(
    slots, received_ref, signs_ref, inv_noise_ref, inner_cos_ref, inner_sin_ref, outer_a_ref,
    outer_s_ref, send_ref, weighted_ref, scalars_ref, signs_folded, noise_folded, sums_ref,
    mapped_ref,
):
    places = send_ref.shape[0]
    probes = received_ref.shape[0] // places
    cycles = inv_noise_ref.shape[0]
    outer = signs_folded.shape[0] // cycles
    rows = probes * 2
    width = slots * rows
    own = lax.axis_index("probe")

    received = received_ref[:places]
    for p in range(1, probes):
        received = received + received_ref[p * places : (p + 1) * places]
    scalars_ref[...] = jnp.broadcast_to(
        jnp.sum(received, axis=0, keepdims=True), scalars_ref.shape
    )
    for s in range(slots):
        sums_ref[pl.ds(s, places, stride=slots), :] = turn(received, -s * rows)
    coeffs = sums_ref[...]
    count = coeffs.shape[0]
    fold(signs_ref.at[0], signs_folded)
    fold(inv_noise_ref, noise_folded)
    inner_cos, inner_sin = inner_cos_ref[...], inner_sin_ref[...]
    lane = iota((count, LANES), 1)
    acc = jnp.zeros((count, LANES), F32)
    totals = [jnp.zeros((1, LANES), F32) for _ in range(probes)]
    for f in range(cycles):
        high, low = [], []
        for p in range(probes):
            base = f * width + p * 2
            cos_coeff, sin_coeff = coeffs[:, base : base + 1], coeffs[:, base + 1 : base + 2]
            real = cos_coeff * inner_cos + sin_coeff * inner_sin
            imag = cos_coeff * inner_sin - sin_coeff * inner_cos
            hi, lo = halves(jnp.concatenate([real, imag], axis=0))
            high.append(hi)
            low.append(lo)
        high = jnp.concatenate(high, axis=1)
        low = jnp.concatenate(low, axis=1)
        mapped = dot(outer_s_ref[...], high)
        mapped = mapped[:outer] + mapped[outer:] + dot(outer_s_ref[:outer, :], low)
        mapped_ref[...] = mapped
        picked = mapped_ref[:, pl.ds(pl.multiple_of(own * LANES, LANES), LANES)]
        weighted_ref[pl.ds(f, outer, stride=cycles), :] = (
            picked * signs_folded[pl.ds(f, outer, stride=cycles), :]
        )
        noise = noise_folded[pl.ds(f, outer, stride=cycles), :]
        pixels = jnp.concatenate([noise] * probes, axis=1) * mapped
        power = jnp.sum(pixels * mapped, axis=0, keepdims=True)
        for p in range(probes):
            totals[p] = totals[p] + power[:, p * LANES : (p + 1) * LANES]
        hi, lo = halves(pixels)
        table_hi = outer_a_ref[:, :outer]
        parts = dot(table_hi, hi) + dot(table_hi, lo) + dot(
            outer_a_ref[:, LANES : LANES + outer], hi
        )
        for p in range(probes):
            acc = twiddle_sums(
                parts[:, p * LANES : (p + 1) * LANES], inner_cos, inner_sin, acc, lane,
                f * width + p * 2,
            )
    sums_ref[...] = acc
    out = join_slots(sums_ref, slots, rows)
    lane = iota((1, LANES), 1)
    for p in range(probes):
        value = jnp.sum(totals[p], axis=1, keepdims=True)
        out = out + jnp.where(lane == SCALARS + p, value, 0.0)
    send_ref[...] = out


def fourth_kernel(
    slots, orders_ref, received_ref, rows_ref, inv_signal_ref, legendre_ref, terms_ref,
    weighted_ref, scalars_ref, send_ref, stack_ref,
):
    probes = send_ref.shape[0]
    quarter = legendre_ref.shape[1]
    rows = probes * 2
    blocks = quarter // LANES
    own = lax.axis_index("probe")
    first_slot = lax.axis_index("sky") * slots
    received = received_ref[...]
    columns, _ = latitude_columns(received, rows_ref, slots, probes, stack_ref)
    first_degree = own * quarter
    signal = inv_signal_ref[:, pl.ds(pl.multiple_of(first_degree, LANES), quarter)]
    row, lane = iota((rows, LANES), 0), iota((rows, LANES), 1)

    def column(line, base):
        return jnp.sum(jnp.where(lane == base + row // 2, line, 0.0), axis=1, keepdims=True)

    noise_part = column(jnp.sum(received, axis=0, keepdims=True), SCALARS)
    norm = column(scalars_ref[:1], SCALARS)
    prior = column(scalars_ref[:1], SCALARS + probes)
    ratio = norm / (prior + noise_part)
    own_ratio = jnp.sum(
        jnp.where(iota((rows, 1), 0) == own * 2, ratio, 0.0), axis=0, keepdims=True
    )
    weighted = weighted_ref[...] * own_ratio
    for p in range(probes):
        send_ref[p, blocks * slots * 2 :, :] = weighted
    for k in range(slots):
        leg_hi, leg_lo = halves(legendre_ref[k])
        noise_terms = degree_sums(
            leg_hi, leg_lo, columns, k, slots, probes, orders_ref[first_slot + k], first_degree
        )
        terms = terms_ref[k]
        residual = terms - ratio * (signal * terms + noise_terms)
        for p in range(probes):
            for b in range(blocks):
                send_ref[p, pl.ds((b * slots + k) * 2, 2), :] = residual[
                    p * 2 : p * 2 + 2, b * LANES : (b + 1) * LANES
                ]


def last_kernel(received_ref, residual_ref, variance_ref):
    probes = received_ref.shape[0]
    slots = residual_ref.shape[1]
    quarter = residual_ref.shape[3] // probes
    blocks = quarter // LANES
    cycles, length = variance_ref.shape
    start = blocks * slots * 2
    total = received_ref[0, start:, :]
    for p in range(1, probes):
        total = total + received_ref[p, start:, :]
    total = total * (1.0 / probes)
    for j in range(length // LANES):
        variance_ref[:, j * LANES : (j + 1) * LANES] = total[j * cycles : (j + 1) * cycles]
    for x in range(probes):
        for b in range(blocks):
            for k in range(slots):
                place = x * quarter + b * LANES
                residual_ref[0, k, :, place : place + LANES] = received_ref[
                    x, pl.ds((b * slots + k) * 2, 2), :
                ]


def call(kernel, outs, scratch, in_smem, args, name):
    vmem = pl.BlockSpec(memory_space=pltpu.VMEM)
    smem = pl.BlockSpec(memory_space=pltpu.SMEM)
    return pl.pallas_call(
        kernel,
        out_shape=[jax.ShapeDtypeStruct(shape, dtype) for shape, dtype in outs],
        in_specs=[smem if i in in_smem else vmem for i in range(len(args))],
        out_specs=[vmem] * len(outs),
        scratch_shapes=[pltpu.VMEM(shape, dtype) for shape, dtype in scratch],
        compiler_params=pltpu.CompilerParams(vmem_limit_bytes=VMEM_BYTES),
        name=name,
    )(*args)


def per_device(legendre, signs, inv_noise, inv_signal, harmonic_order_values, cycle_rows):
    slots, quarter, total = legendre.shape
    _, cycles, length = signs.shape
    probes = lax.axis_size("probe")
    places = lax.axis_size("sky")
    count = harmonic_order_values.shape[0]
    outer = length // LANES
    rows = probes * 2
    orders = harmonic_order_values
    order_row = orders.reshape(1, count)
    row_line = cycle_rows.reshape(1, total)
    signal_line = inv_signal.reshape(1, probes * quarter)

    def everywhere(send):
        return lax.all_to_all(
            send.reshape(probes * places, LANES), ("probe", "sky"), 0, 0, tiled=True
        )

    send, inner_cos, inner_sin, outer_a, outer_s = call(
        functools.partial(first_kernel, slots),
        [
            ((probes, places, LANES), F32),
            ((count, LANES), F32),
            ((count, LANES), F32),
            ((2 * count, 2 * LANES), BF16),
            ((2 * outer, 2 * count), BF16),
        ],
        [((outer * cycles, LANES), F32), ((count, LANES), F32)],
        (),
        (order_row, signs),
        "cycle_sums",
    )
    received = everywhere(send)
    send, terms = call(
        functools.partial(second_kernel, slots),
        [((probes, places, LANES), F32), ((slots, rows, quarter), F32)],
        [((total, LANES), F32), ((total, LANES), F32)],
        (0,),
        (orders, received, row_line, signal_line, legendre),
        "degrees_there_and_back",
    )
    received = everywhere(send)
    send, weighted, scalars = call(
        functools.partial(third_kernel, slots),
        [((places, LANES), F32), ((outer * cycles, LANES), F32), ((8, LANES), F32)],
        [
            ((outer * cycles, LANES), F32),
            ((outer * cycles, LANES), F32),
            ((count, LANES), F32),
            ((outer, probes * LANES), F32),
        ],
        (),
        (received, signs, inv_noise, inner_cos, inner_sin, outer_a, outer_s),
        "cycles_there_and_back",
    )
    received = lax.all_to_all(send, "sky", 0, 0, tiled=True)
    height = quarter // LANES * slots * 2 + outer * cycles
    (send,) = call(
        functools.partial(fourth_kernel, slots),
        [((probes, height, LANES), F32)],
        [((total, LANES), F32)],
        (0,),
        (orders, received, row_line, signal_line, legendre, terms, weighted, scalars),
        "residual_terms",
    )
    received = lax.all_to_all(send, "probe", 0, 0, tiled=True)
    residual, variance = call(
        last_kernel,
        [((1, slots, 2, probes * quarter), F32), ((cycles, length), F32)],
        [],
        (),
        (received,),
        "outputs",
    )
    return residual, variance


def solution(mesh):
    in_specs = (P("sky", "probe", None), P("probe", "sky", None), P("sky", None), P(), P(), P())
    out_specs = (P("probe", "sky", None, None), P("sky", None))
    return jax.shard_map(
        per_device, mesh=mesh, in_specs=in_specs, out_specs=out_specs, check_vma=False
    )
```

time: 355 us -> 115 us (0.32)
  waiting for transfers between devices: 70.9 us -> 0 us
  blocking collectives: 164 us -> 94.4 us
  local copies, waits for them, and re-layouts: 39 us -> 5.17 us
  starting transfers between devices: 32.3 us -> 0 us
  matrix products: 21 us -> 0 us
  Pallas kernels: 0 us -> 14.4 us
  between operations: 14.3 us -> 0.66 us
  other arithmetic: 12.2 us -> 0 us
    psum x1 -> x0, blocking collectives: 98.7 us -> none  [total_norm_value(): return lax.psum(local_terms, ('probe', 'sky'))]
    all_to_all x1 -> x4, blocking collectives: 32.4 us -> 94.4 us  [the longest x2 64.8 us: everywhere(): lax.all_to_all(send.reshape(probes * places, LANES), ('probe', 'sky'), 0,...]
    psum x1 -> x0, waiting for transfers between devices: 42 us -> none  [per_device(): variance = lax.psum(own_ratio * weighted, 'probe') / probe_count]
    all_to_all x4 -> x0, starting transfers between devices: 32.3 us -> none  [the longest x2 25.7 us: cycle_analysis(): lax.all_to_all(harmonic_coefficient_set, 'sky', split_axis=0, concat_axis...]
    all_to_all x4 -> x0, waiting for transfers between devices: 28.8 us -> none  [the longest x2 24.4 us: cycle_analysis(): lax.all_to_all(harmonic_coefficient_set, 'sky', split_axis=0, concat_axis...]
    scatter x4 -> x0, local copies, waits for them, and re-layouts: 27.5 us -> none  [cycle_analysis(): return jnp.zeros_like(local_orders).at[:, :, cycle_rows].set(local_orders)]
    dot_general x9 -> x0, matrix products: 21 us -> none  [the longest x2 11.5 us: degree_terms(): jnp.einsum('klr,pkcr->pkcl', masked_sky_map, lax.all_gather(latitude[None...]
    all_gather x2 -> x0, blocking collectives: 19.1 us -> none  [degree_terms(): lax.all_gather(latitude[None], 'probe', axis=0, tiled=True)]
  transfers between devices with their start and end apart: 5 -> 0, of which waited for: 4 -> 0; matrix products, arithmetic and copies ran while one was open for 7% -> 0% of each run, Pallas kernels for 0% -> 0%
where the time goes in v1:
time: 115 us
  blocking collectives  94.4 us (82%)
  Pallas kernels  14.4 us (13%)
  local copies, waits for them, and re-layouts  5.17 us (4%)
    all_to_all x2, blocking collectives, everywhere(): lax.all_to_all(send.reshape(probes * places, LANES), ('probe', 'sky'), 0,...  64.8 us
    all_to_all x1, blocking collectives, per_device(): received = lax.all_to_all(send, 'sky', 0, 0, tiled=True)  17.5 us
    pallas_call x5, Pallas kernels, call(): pl.pallas_call(kernel, out_shape=[jax.ShapeDtypeStruct(shape, dtype) for...  14.4 us
    all_to_all x1, blocking collectives, per_device(): received = lax.all_to_all(send, 'probe', 0, 0, tiled=True)  12 us
    unnamed x16, local copies, waits for them, and re-layouts  5.17 us

profile of v1, /device:TPU:1, one launch (start us, length us, event | category | flops | bytes accessed | tf_op | source)
XLA Modules:
  0.0 114.6 jit_solution(4289570214545304467)
XLA Ops:
  0.6 0.0 copy-start.2
  0.6 0.9 copy-done.2
  1.5 0.0 copy-start.6
  1.5 0.7 copy-done.6
  2.2 0.0 copy-start.3
  2.2 0.0 copy-start.4
  2.2 2.1 %cycle_sums.1 = (f32[4,128,128]{2,1,0:T(8,128)S(1)}, f32[256,128]{1,0:T(8,128)S(1)}, f32[256,128]{1,0:T(8,128)S(1)}, bf16[512,256]{1,0:T(8,128)(2,1)S(1)}, bf16[128,512]{1,0:T(8,128)(2,1)S(1)}) custom-call(s32[1,256]{1,0:T(1,128)S(1)} %bitcast.23, s32[1,4,8192]{2,1,0:T(4,128)S(1)} %copy-done.2), custom_call_target="tpu_custom_call" | custom-call | tf_op jit(solution)/shard_map/cycle_sums/pallas_call | solution.py:343
  4.3 38.8 %all_to_all.38 = f32[512,1,128]{2,1,0:T(1,128)S(1)} all-to-all(f32[512,1,128]{2,1,0:T(1,128)S(1)} %bitcast.18), channel_id=1, replica_groups=mesh['probe'=4,'sky'=128] {'probe','sky'}, dimensions={0} | all-to-all | bytes 524288 | tf_op jit(solution)/shard_map/all_to_all | solution.py:368
  43.1 0.0 copy-start
  43.1 2.2 %copy-done = f32[2,1024,512]{2,1,0:T(8,128)S(1)} copy-done((f32[2,1024,512]{2,1,0:T(8,128)S(1)}, f32[2,1024,512]{2,1,0:T(8,128)}, u32[]{:S(2)}) %copy-start) | copy-done | bytes 4194328
  45.3 0.0 copy-start.5
  45.3 0.7 copy-done.5
  46.0 0.0 copy-start.7
  46.0 0.7 copy-done.7
  46.7 0.0 copy-start.1
  46.7 4.9 %degrees_there_and_back.1 = (f32[4,128,128]{2,1,0:T(8,128)S(1)}, f32[2,8,1024]{2,1,0:T(8,128)S(1)}) custom-call(s32[256]{0:T(256)S(1)} %copy-done.6, f32[512,128]{1,0:T(8,128)S(1)} %bitcast.15, s32[1,512]{1,0:T(1,128)S(1)} %bitcast.24, f32[1,4096]{1,0:T(1,128)S(1)} %bitcast.20, f32[2,1024,512]{2,1,0:T(8,128)S(1)} %copy-done), custom_call_target="tpu_custom_call" | custom-call | tf_op jit(solution)/shard_map/degrees_there_and_back/pallas_call | solution.py:343
  51.6 26.0 %all_to_all.39 = f32[512,1,128]{2,1,0:T(1,128)S(1)} all-to-all(f32[512,1,128]{2,1,0:T(1,128)S(1)} %bitcast.19), channel_id=1, replica_groups=mesh['probe'=4,'sky'=128] {'probe','sky'}, dimensions={0} | all-to-all | bytes 524288 | tf_op jit(solution)/shard_map/all_to_all | solution.py:368
  77.7 0.0 copy-done.3
  77.7 0.0 copy-done.4
  77.7 4.4 %cycles_there_and_back.1 = (f32[128,128]{1,0:T(8,128)S(1)}, f32[256,128]{1,0:T(8,128)S(1)}, f32[8,128]{1,0:T(8,128)S(1)}) custom-call(f32[512,128]{1,0:T(8,128)S(1)} %bitcast.16, s32[1,4,8192]{2,1,0:T(4,128)S(1)} %copy-done.3, f32[4,8192]{1,0:T(4,128)S(1)} %copy-done.4, f32[256,128]{1,0:T(8,128)S(1)} %get-tuple-element.14.inner_cos_ref, ...), custom_call_target="tpu_custom_call" | custom-call | tf_op jit(solution)/shard_map/cycles_there_and_back/pallas_call | solution.py:343
  82.1 17.5 %all_to_all.40 = f32[128,1,128]{2,1,0:T(1,128)S(1)} all-to-all(f32[128,1,128]{2,1,0:T(1,128)S(1)} %bitcast.22), channel_id=1, replica_groups=mesh['probe'=4,'sky'=128] {'sky'}, dimensions={0} | all-to-all | bytes 131072 | tf_op jit(solution)/shard_map/all_to_all | solution.py:409
  99.6 0.0 copy-done.1
  99.6 2.3 %residual_terms.1 = f32[4,288,128]{2,1,0:T(8,128)S(1)} custom-call(s32[256]{0:T(256)S(1)} %copy-done.6, f32[128,128]{1,0:T(8,128)S(1)} %bitcast.17, s32[1,512]{1,0:T(1,128)S(1)} %bitcast.25, f32[1,4096]{1,0:T(1,128)S(1)} %bitcast.21, f32[2,1024,512]{2,1,0:T(8,128)S(1)} %copy-done.1, f32[2,8,1024]{2,1,0:T(8,128)S(1)} %get-tuple-element.19.terms_ref, ...), custom_call_target="tpu_custom_call" | custom-call | tf_op jit(solution)/shard_map/residual_terms/pallas_call | solution.py:343
  101.9 12.0 %all_to_all.41.received_ref = f32[4,288,128]{2,1,0:T(8,128)S(1)} all-to-all(f32[4,288,128]{2,1,0:T(8,128)S(1)} %residual_terms.1), channel_id=1, replica_groups=mesh['probe'=4,'sky'=128] {'probe'}, dimensions={0} | all-to-all | bytes 1179648 | tf_op jit(solution)/shard_map/all_to_all | solution.py:419
  113.9 0.7 outputs.1
Async XLA Ops:
  0.6 0.9 copy-start.2
  1.5 0.7 copy-start.6
  2.2 75.4 %copy-start.3 = (s32[1,4,8192]{2,1,0:T(4,128)S(1)}, s32[1,4,8192]{2,1,0:T(4,128)}, u32[]{:S(2)}) copy-start(s32[1,4,8192]{2,1,0:T(4,128)} %signs_ref.3) | copy-start | bytes 393220
  2.2 75.4 %copy-start.4 = (f32[4,8192]{1,0:T(4,128)S(1)}, f32[4,8192]{1,0:T(4,128)}, u32[]{:S(2)}) copy-start(f32[4,8192]{1,0:T(4,128)} %inv_noise_ref.1) | copy-start | bytes 393220
  43.1 2.2 %copy-start = (f32[2,1024,512]{2,1,0:T(8,128)S(1)}, f32[2,1024,512]{2,1,0:T(8,128)}, u32[]{:S(2)}) copy-start(f32[2,1024,512]{2,1,0:T(8,128)} %legendre_ref.3) | copy-start | bytes 12582916
  45.3 0.7 copy-start.5
  46.0 0.7 copy-start.7
  46.7 52.9 %copy-start.1 = (f32[2,1024,512]{2,1,0:T(8,128)S(1)}, f32[2,1024,512]{2,1,0:T(8,128)}, u32[]{:S(2)}) copy-start(f32[2,1024,512]{2,1,0:T(8,128)} %legendre_ref.3) | copy-start | bytes 12582916

commit v2 on v1

v2 whole, which is shorter than its diff:
```python
import functools
import math

import jax
import jax.numpy as jnp
from jax import lax
from jax.experimental import pallas as pl
from jax.experimental.pallas import tpu as pltpu
from jax.sharding import PartitionSpec as P

F32 = jnp.float32
BF16 = jnp.bfloat16
LANES = 128
SCALARS = 64
VMEM_BYTES = 24 * 1024 * 1024


def iota(shape, dim):
    return lax.broadcasted_iota(jnp.int32, shape, dim)


def dot(a, b):
    return jnp.dot(a, b, preferred_element_type=F32)


def halves(value):
    high = value.astype(BF16)
    return high, (value - high.astype(F32)).astype(BF16)


def turn(value, lanes):
    lanes = lanes % LANES
    return pltpu.roll(value, lanes, 1) if lanes else value


def fold(flat_ref, folded_ref):
    cycles = flat_ref.shape[-2]
    for j in range(folded_ref.shape[0] // cycles):
        folded_ref[j * cycles : (j + 1) * cycles, :] = flat_ref[
            :, j * LANES : (j + 1) * LANES
        ].astype(F32)


def twiddle_sums(parts, inner_cos, inner_sin, acc, lane, base):
    count = inner_cos.shape[0]
    real, imag = parts[:count], parts[count:]
    cos_sum = jnp.sum(inner_cos * real - inner_sin * imag, axis=1, keepdims=True)
    sin_sum = jnp.sum(inner_sin * real + inner_cos * imag, axis=1, keepdims=True)
    acc = jnp.where(lane == base, cos_sum, acc)
    return jnp.where(lane == base + 1, sin_sum, acc)


def gather_rows(by_row_ref, places, shifts):
    out = by_row_ref[pl.ds(0, places, stride=len(shifts)), :]
    for s in range(1, len(shifts)):
        out = out + turn(by_row_ref[pl.ds(s, places, stride=len(shifts)), :], shifts[s])
    return out


def own_half(received_ref, source, groups):
    places = received_ref.shape[1] // groups
    total = received_ref[source, :places]
    for g in range(1, groups):
        total = total + received_ref[source, g * places : (g + 1) * places]
    return jnp.where(lax.axis_index("core") == 0, total, turn(total, LANES // 2))


def first_kernel(
    slots, orders_hbm, signs_hbm, rows_hbm, signal_hbm, noise_hbm, legendre_hbm,
    send_ref, inner_cos_ref, inner_sin_ref, outer_a_ref, outer_s_ref, limits_ref, signs_ref,
    rows_ref, signal_ref, noise_ref, legendre_ref,
    orders_ref, folded_ref, sums_ref, sems,
):
    count = orders_ref.shape[1]
    probes, places = send_ref.shape[:2]
    cycles = signs_ref.shape[1]
    outer = folded_ref.shape[0] // cycles
    cycle_length = outer * LANES
    cores = count // slots // places
    own = lax.axis_index("probe")
    quarter = signal_ref.shape[1]
    own_signal = signal_hbm.at[:, pl.ds(pl.multiple_of(own * quarter, LANES), quarter)]

    copies = [
        pltpu.make_async_copy(source, target, sems.at[n])
        for n, (source, target) in enumerate(
            [
                (orders_hbm, orders_ref),
                (signs_hbm, signs_ref),
                (rows_hbm, rows_ref),
                (own_signal, signal_ref),
                (noise_hbm, noise_ref),
                (legendre_hbm, legendre_ref),
            ]
        )
    ]
    for copy in copies:
        copy.start()
    copies[0].wait()

    order_row = orders_ref[...]
    first_slot = (lax.axis_index("place") * cores + lax.axis_index("core")) * slots
    for k in range(slots):
        picked = jnp.where(iota((1, count), 1) == first_slot + k, order_row, 0).astype(F32)
        picked = jnp.sum(picked, axis=1, keepdims=True).astype(jnp.int32)
        limits_ref[k : k + 1, :] = jnp.broadcast_to(picked, (1, LANES))
    order_col = jnp.sum(
        jnp.where(iota((count, count), 0) == iota((count, count), 1), order_row.astype(F32), 0.0),
        axis=1,
        keepdims=True,
    ).astype(jnp.int32)
    inner_angles = ((order_col * iota((count, LANES), 1)) & (cycle_length - 1)).astype(F32) * (
        2.0 * math.pi / cycle_length
    )
    scale_factor = 1.0 / math.sqrt(cycle_length)
    inner_cos = jnp.cos(inner_angles) * scale_factor
    inner_sin = jnp.sin(inner_angles) * scale_factor
    inner_cos_ref[...] = inner_cos
    inner_sin_ref[...] = inner_sin
    step = 2.0 * math.pi / outer
    twice = ((order_col * iota((count, LANES), 1)) & (outer - 1)).astype(F32) * step
    cos_hi, cos_lo = halves(jnp.cos(twice))
    sin_hi, sin_lo = halves(jnp.sin(twice))
    outer_a_ref[:count, :LANES] = cos_hi
    outer_a_ref[:count, LANES:] = cos_lo
    outer_a_ref[count:, :LANES] = sin_hi
    outer_a_ref[count:, LANES:] = sin_lo
    across = ((order_row * iota((outer, count), 0)) & (outer - 1)).astype(F32) * step
    cos_hi, cos_lo = halves(jnp.cos(across))
    sin_hi, sin_lo = halves(-jnp.sin(across))
    outer_s_ref[:outer, :count] = cos_hi
    outer_s_ref[:outer, count:] = sin_hi
    outer_s_ref[outer:, :count] = cos_lo
    outer_s_ref[outer:, count:] = sin_lo

    copies[1].wait()
    fold(signs_ref.at[0], folded_ref)
    pixels = jnp.concatenate(
        [folded_ref[pl.ds(f, outer, stride=cycles), :] for f in range(cycles)], axis=1
    ).astype(BF16)
    parts = dot(outer_a_ref[:, :outer], pixels) + dot(
        outer_a_ref[:, LANES : LANES + outer], pixels
    )
    lane = iota((count, LANES), 1)
    acc = jnp.zeros((count, LANES), F32)
    rows = probes * 2
    for f in range(cycles):
        acc = twiddle_sums(
            parts[:, f * LANES : (f + 1) * LANES], inner_cos, inner_sin, acc, lane,
            f * slots * rows + own * 2,
        )
    sums_ref[...] = acc
    shifts = [c * (LANES // 2) + k * rows for c in range(cores) for k in range(slots)]
    out = gather_rows(sums_ref, places, shifts)
    for p in range(probes):
        send_ref[p] = out
    for copy in copies[2:]:
        copy.wait()


def latitude_columns(received, cores, rows_ref, width, stack_ref):
    total = rows_ref.shape[1]
    for c in range(cores):
        values = received(c)
        places = values.shape[0]
        cycles = total // (places * cores)
        lane = iota((places, LANES), 1)
        for f in range(cycles):
            value = turn(values, -f * width)
            high = value.astype(BF16).astype(F32)
            low = turn(value - high, width)
            stack_ref[pl.ds(c * cycles + f, places, stride=cores * cycles), :] = jnp.where(
                lane < width, high, jnp.where(lane < 2 * width, low, 0.0)
            )
    chosen = jnp.where(iota((total, total), 0) == rows_ref[...], 1.0, 0.0).astype(BF16)
    return dot(chosen, stack_ref[...].astype(BF16)).astype(BF16), chosen


def degree_sums(leg_hi, leg_lo, columns, k, rows, width, order, first_degree):
    across = (dot(leg_hi, columns) + dot(leg_lo, columns)).T
    terms = across[k * rows : (k + 1) * rows] + across[
        width + k * rows : width + (k + 1) * rows
    ]
    degrees = first_degree + iota(terms.shape, 1)
    return jnp.where(degrees >= order, terms, 0.0)


def second_kernel(
    received_ref, rows_ref, signal_ref, limits_ref, legendre_ref,
    send_ref, terms_ref, scalars_ref, hi_ref, lo_ref, stack_ref, spread_ref,
):
    cores = received_ref.shape[0]
    probes, places = send_ref.shape[:2]
    slots, quarter, total = legendre_ref.shape
    cycles = total // (places * cores)
    rows = probes * 2
    width = slots * rows
    columns, chosen = latitude_columns(
        lambda c: own_half(received_ref, c, probes), cores, rows_ref, width, stack_ref
    )
    first_degree = lax.axis_index("probe") * quarter
    signal = signal_ref[...]
    norm = jnp.zeros((rows, 1), F32)
    prior = jnp.zeros((rows, 1), F32)
    fields = []
    for k in range(slots):
        leg_hi, leg_lo = halves(legendre_ref[k])
        hi_ref[k] = leg_hi
        lo_ref[k] = leg_lo
        terms = degree_sums(
            leg_hi, leg_lo, columns, k, rows, width, limits_ref[k : k + 1, :1], first_degree
        )
        terms_ref[k] = terms
        squares = terms * terms
        norm = norm + jnp.sum(squares, axis=1, keepdims=True)
        prior = prior + jnp.sum(squares * signal, axis=1, keepdims=True)
        both = jnp.concatenate(halves(terms), axis=0)
        field = dot(both, leg_hi) + dot(both, leg_lo)
        fields.append(field[:rows] + field[rows:])
    fields = jnp.concatenate(fields, axis=0)
    both = jnp.concatenate(halves(fields), axis=0)
    by_cycle = dot(both, chosen)
    by_cycle = by_cycle[:width] + by_cycle[width:]
    spread_ref[...] = jnp.concatenate(
        [by_cycle, jnp.zeros((LANES - width, total), F32)], axis=0
    ).T
    out = gather_rows(spread_ref, places, [s * width for s in range(cores * cycles)])
    for p in range(probes):
        send_ref[p] = out
    row, lane = iota((rows, LANES), 0), iota((rows, LANES), 1)
    scalars = jnp.where(lane == SCALARS + row // 2, norm, 0.0)
    scalars = scalars + jnp.where(lane == SCALARS + probes + row // 2, prior, 0.0)
    scalars_ref[...] = jnp.broadcast_to(
        jnp.sum(scalars, axis=0, keepdims=True), scalars_ref.shape
    )


def third_kernel(
    slots, received_ref, signs_ref, inv_noise_ref, inner_cos_ref, inner_sin_ref, outer_a_ref,
    outer_s_ref, scalars_ref, send_ref, weighted_ref, signs_folded, noise_folded, sums_ref,
    mapped_ref,
):
    cores = received_ref.shape[0]
    all_places = send_ref.shape[0]
    places = all_places // cores
    probes = received_ref.shape[1] // places
    cycles = inv_noise_ref.shape[0]
    outer = signs_folded.shape[0] // cycles
    rows = probes * 2
    width = slots * rows
    own = lax.axis_index("probe")

    for c in range(cores):
        received = own_half(received_ref, c, probes)
        for k in range(slots):
            sums_ref[pl.ds(c * slots + k, places, stride=cores * slots), :] = turn(
                received, -k * rows
            )
    coeffs = sums_ref[...]
    count = coeffs.shape[0]
    fold(signs_ref.at[0], signs_folded)
    fold(inv_noise_ref, noise_folded)
    inner_cos, inner_sin = inner_cos_ref[...], inner_sin_ref[...]
    lane = iota((count, LANES), 1)
    acc = jnp.zeros((count, LANES), F32)
    totals = [jnp.zeros((1, LANES), F32) for _ in range(probes)]
    for f in range(cycles):
        high, low = [], []
        for p in range(probes):
            base = f * width + p * 2
            cos_coeff, sin_coeff = coeffs[:, base : base + 1], coeffs[:, base + 1 : base + 2]
            real = cos_coeff * inner_cos + sin_coeff * inner_sin
            imag = cos_coeff * inner_sin - sin_coeff * inner_cos
            hi, lo = halves(jnp.concatenate([real, imag], axis=0))
            high.append(hi)
            low.append(lo)
        high = jnp.concatenate(high, axis=1)
        low = jnp.concatenate(low, axis=1)
        mapped = dot(outer_s_ref[...], high)
        mapped = mapped[:outer] + mapped[outer:] + dot(outer_s_ref[:outer, :], low)
        mapped_ref[...] = mapped
        picked = mapped_ref[:, pl.ds(pl.multiple_of(own * LANES, LANES), LANES)]
        weighted_ref[pl.ds(f, outer, stride=cycles), :] = (
            picked * signs_folded[pl.ds(f, outer, stride=cycles), :]
        )
        noise = noise_folded[pl.ds(f, outer, stride=cycles), :]
        pixels = jnp.concatenate([noise] * probes, axis=1) * mapped
        power = jnp.sum(pixels * mapped, axis=0, keepdims=True)
        for p in range(probes):
            totals[p] = totals[p] + power[:, p * LANES : (p + 1) * LANES]
        hi, lo = halves(pixels)
        table_hi = outer_a_ref[:, :outer]
        parts = dot(table_hi, hi) + dot(table_hi, lo) + dot(
            outer_a_ref[:, LANES : LANES + outer], hi
        )
        for p in range(probes):
            acc = twiddle_sums(
                parts[:, p * LANES : (p + 1) * LANES], inner_cos, inner_sin, acc, lane,
                f * width + p * 2,
            )
    sums_ref[...] = acc
    out = gather_rows(sums_ref, all_places, [k * rows for k in range(slots)])
    line = scalars_ref[:1]
    lane = iota((1, LANES), 1)
    for p in range(probes):
        value = jnp.sum(totals[p], axis=1, keepdims=True)
        line = line + jnp.where(lane == SCALARS + 2 * probes + p, value, 0.0)
    send_ref[...] = out + line


def fourth_kernel(
    received_ref, rows_ref, signal_ref, limits_ref, hi_ref, lo_ref, terms_ref, weighted_ref,
    send_ref, stack_ref,
):
    probes = send_ref.shape[0]
    slots, quarter, _ = hi_ref.shape
    rows = probes * 2
    blocks = quarter // LANES
    block_rows = blocks * slots * 2
    received = received_ref[...]
    columns, _ = latitude_columns(lambda c: received, 1, rows_ref, slots * rows, stack_ref)
    first_degree = lax.axis_index("probe") * quarter
    signal = signal_ref[...]
    line = jnp.broadcast_to(jnp.sum(received, axis=0, keepdims=True), (8, LANES))
    for p in range(probes):
        send_ref[p, 2 * block_rows : 2 * block_rows + 8, :] = line
        send_ref[p, 2 * block_rows + 8 :, :] = weighted_ref[...]
    for k in range(slots):
        noise_terms = degree_sums(
            hi_ref[k], lo_ref[k], columns, k, rows, slots * rows, limits_ref[k : k + 1, :1],
            first_degree,
        )
        terms = terms_ref[k]
        image = signal * terms + noise_terms
        for p in range(probes):
            for b in range(blocks):
                place = (b * slots + k) * 2
                own = (slice(p * 2, p * 2 + 2), slice(b * LANES, (b + 1) * LANES))
                send_ref[p, place : place + 2, :] = terms[own]
                send_ref[p, block_rows + place : block_rows + place + 2, :] = image[own]


def last_kernel(received_ref, residual_ref, variance_ref):
    probes = received_ref.shape[0]
    slots = residual_ref.shape[1]
    quarter = residual_ref.shape[3] // probes
    blocks = quarter // LANES
    block_rows = blocks * slots * 2
    cycles, length = variance_ref.shape
    own = lax.axis_index("probe")
    lane = iota((8, LANES), 1)
    lines = [received_ref[p, 2 * block_rows : 2 * block_rows + 8, :] for p in range(probes)]
    degree_line = lines[0]
    for p in range(1, probes):
        degree_line = degree_line + lines[p]

    def ratio(p):
        def value(line, base):
            return jnp.sum(jnp.where(lane == base + p, line, 0.0), axis=1, keepdims=True)

        norm = value(degree_line, SCALARS)
        prior = value(degree_line, SCALARS + probes)
        return norm / (prior + value(lines[0], SCALARS + 2 * probes))

    start = 2 * block_rows + 8
    total = received_ref[0, start:, :] * ratio(0)[:1]
    for p in range(1, probes):
        total = total + received_ref[p, start:, :] * ratio(p)[:1]
    total = total * (1.0 / probes)
    for j in range(length // LANES):
        variance_ref[:, j * LANES : (j + 1) * LANES] = total[j * cycles : (j + 1) * cycles]
    own_ratio = ratio(own)[:1]
    for x in range(probes):
        residual = (
            received_ref[x, :block_rows, :]
            - own_ratio * received_ref[x, block_rows : 2 * block_rows, :]
        )
        for b in range(blocks):
            for k in range(slots):
                place = x * quarter + b * LANES
                row = (b * slots + k) * 2
                residual_ref[0, k, :, place : place + LANES] = residual[row : row + 2]


def call(kernel, outs, scratch, args, name, space=pltpu.VMEM):
    return pl.pallas_call(
        kernel,
        out_shape=[jax.ShapeDtypeStruct(shape, dtype) for shape, dtype in outs],
        in_specs=[pl.BlockSpec(memory_space=space)] * len(args),
        out_specs=[pl.BlockSpec(memory_space=pltpu.VMEM)] * len(outs),
        scratch_shapes=scratch,
        compiler_params=pltpu.CompilerParams(vmem_limit_bytes=VMEM_BYTES),
        name=name,
    )(*args)


def per_device(legendre, signs, inv_noise, inv_signal, harmonic_order_values, cycle_rows):
    slots, quarter, total = legendre.shape
    _, cycles, length = signs.shape
    probes = lax.axis_size("probe")
    places = lax.axis_size("place")
    cores = lax.axis_size("core")
    count = harmonic_order_values.shape[0]
    outer = length // LANES
    rows = probes * 2
    wide = ((total, LANES), F32)
    by_order = ((count, LANES), F32)
    folded = ((outer * cycles, LANES), F32)

    def everywhere(send):
        received = lax.all_to_all(
            send.reshape(probes * places, LANES), ("probe", "place"), 0, 0, tiled=True
        )
        return lax.all_gather(received, "core", axis=0)

    (
        send, inner_cos, inner_sin, outer_a, outer_s, limits, signs_near, row_line, signal,
        noise_near, legendre_near,
    ) = call(
        functools.partial(first_kernel, slots),
        [
            ((probes, places, LANES), F32),
            by_order,
            by_order,
            ((2 * count, 2 * LANES), BF16),
            ((2 * outer, 2 * count), BF16),
            ((8, LANES), jnp.int32),
            (signs.shape, jnp.int32),
            ((1, total), jnp.int32),
            ((1, quarter), F32),
            (inv_noise.shape, F32),
            (legendre.shape, F32),
        ],
        [
            pltpu.VMEM((1, count), jnp.int32),
            pltpu.VMEM(*folded),
            pltpu.VMEM(*by_order),
            pltpu.SemaphoreType.DMA((6,)),
        ],
        (
            harmonic_order_values.reshape(1, count), signs, cycle_rows.reshape(1, total),
            inv_signal.reshape(1, probes * quarter), inv_noise, legendre,
        ),
        "cycle_sums",
        pltpu.HBM,
    )
    received = everywhere(send)
    send, terms, scalars, leg_hi, leg_lo = call(
        second_kernel,
        [
            ((probes, places, LANES), F32),
            ((slots, rows, quarter), F32),
            ((8, LANES), F32),
            (legendre.shape, BF16),
            (legendre.shape, BF16),
        ],
        [pltpu.VMEM(*wide), pltpu.VMEM(*wide)],
        (received, row_line, signal, limits, legendre_near),
        "degrees_there_and_back",
    )
    received = everywhere(send)
    send, weighted = call(
        functools.partial(third_kernel, slots),
        [((places * cores, LANES), F32), folded],
        [
            pltpu.VMEM(*folded),
            pltpu.VMEM(*folded),
            pltpu.VMEM(*by_order),
            pltpu.VMEM((outer, probes * LANES), F32),
        ],
        (
            received, signs_near, noise_near, inner_cos, inner_sin, outer_a, outer_s, scalars,
        ),
        "cycles_there_and_back",
    )
    received = lax.all_to_all(send, ("place", "core"), 0, 0, tiled=True)
    height = quarter // LANES * slots * 4 + 8 + outer * cycles
    (send,) = call(
        fourth_kernel,
        [((probes, height, LANES), F32)],
        [pltpu.VMEM(*wide)],
        (received, row_line, signal, limits, leg_hi, leg_lo, terms, weighted),
        "image_terms",
    )
    received = lax.all_to_all(send, "probe", 0, 0, tiled=True)
    return call(
        last_kernel,
        [((1, slots, 2, probes * quarter), F32), ((cycles, length), F32)],
        [],
        (received,),
        "outputs",
    )


def solution(mesh):
    cores = 2
    split = jax.sharding.Mesh(
        mesh.devices.reshape(mesh.shape["probe"], -1, cores), ("probe", "place", "core")
    )
    sky = ("place", "core")
    in_specs = (P(sky, "probe", None), P("probe", sky, None), P(sky, None), P(), P(), P())
    out_specs = (P("probe", sky, None, None), P(sky, None))

    def run(*args):
        return tuple(
            jax.shard_map(
                per_device, mesh=split, in_specs=in_specs, out_specs=out_specs, check_vma=False
            )(*args)
        )

    return run
```

time: 115 us -> 114 us (level)
  blocking collectives: 94.4 us -> 92 us
    all_to_all x3, blocking collectives: 82.3 us -> 72.4 us  [the longest x2 55.9 us: everywhere(): lax.all_to_all(send.reshape(probes * places, LANES), ('probe', 'place'),...]
    all_gather x0 -> x2, blocking collectives: none -> 7.16 us  [everywhere(): return lax.all_gather(received, 'core', axis=0)]
    unnamed x16 -> x12, local copies, waits for them, and re-layouts: 5.17 us -> 6.06 us
where the time goes in v2:
time: 114 us; the launch traced here: 113 us
  blocking collectives  92 us (81%)
  Pallas kernels  14.3 us (13%)
  local copies, waits for them, and re-layouts  6.06 us (5%)
    all_to_all x2, blocking collectives, everywhere(): lax.all_to_all(send.reshape(probes * places, LANES), ('probe', 'place'),...  55.9 us
    all_to_all x1, blocking collectives, per_device(): received = lax.all_to_all(send, ('place', 'core'), 0, 0, tiled=True)  16.6 us
    pallas_call x5, Pallas kernels, call(): pl.pallas_call(kernel, out_shape=[jax.ShapeDtypeStruct(shape, dtype) for...  14.3 us
    all_to_all x1, blocking collectives, per_device(): received = lax.all_to_all(send, 'probe', 0, 0, tiled=True)  12.4 us
    all_gather x2, blocking collectives, everywhere(): return lax.all_gather(received, 'core', axis=0)  7.16 us
    unnamed x12, local copies, waits for them, and re-layouts  6.06 us

profile of v2, /device:TPU:1, one launch (start us, length us, event | category | flops | bytes accessed | tf_op | source)
XLA Modules:
  0.0 113.0 jit_solution(6119679583409747423)
XLA Ops:
  0.6 0.0 copy-start
  0.6 2.2 %copy-done = f32[2,1024,512]{2,1,0:T(8,128)S(1)} copy-done((f32[2,1024,512]{2,1,0:T(8,128)S(1)}, f32[2,1024,512]{2,1,0:T(8,128)}, u32[]{:S(2)}) %copy-start) | copy-done | bytes 4194328
  2.8 0.0 copy-start.1
  2.8 0.9 copy-done.1
  3.7 0.0 copy-start.2
  3.7 0.9 copy-done.2
  4.6 0.0 copy-start.3
  4.6 0.7 copy-done.3
  5.3 0.0 copy-start.4
  5.3 0.7 copy-done.4
  6.0 0.0 copy-start.5
  6.0 0.7 copy-done.5
  6.7 3.0 %cycle_sums.1 = (f32[4,64,128]{2,1,0:T(8,128)S(1)}, f32[256,128]{1,0:T(8,128)S(1)}, f32[256,128]{1,0:T(8,128)S(1)}, bf16[512,256]{1,0:T(8,128)(2,1)S(1)}, bf16[1...) custom-call(s32[1,256]{1,0:T(1,128)S(1)} %bitcast.23, ...), custom_call_target="tpu_custom_call" | custom-call | tf_op jit(solution)/shard_map/cycle_sums/pallas_call | solution.py:386
  9.7 34.9 %all_to_all.34 = f32[256,1,128]{2,1,0:T(1,128)S(1)} all-to-all(f32[256,1,128]{2,1,0:T(1,128)S(1)} %bitcast.18), channel_id=1, replica_groups=mesh['probe'=4,'place'=64,'core'=2] {'probe','place'}, dimensions={0} | all-to-all | bytes 262144 | tf_op jit(solution)/shard_map/all_to_all | solution.py:411
  44.6 3.9 %all-gather = f32[512,1,128]{2,1,0:T(1,128)S(1)} all-gather(f32[256,1,128]{2,1,0:T(1,128)S(1)} %all_to_all.34), channel_id=2, replica_groups=mesh['probe'=4,'place'=64,'core'=2] {'core'}, dimensions={0}, use_global_device_ids=true | all-gather | bytes 393216 | tf_op jit(solution)/shard_map/all_gather | solution.py:414
  48.4 4.5 %degrees_there_and_back.1 = (f32[4,64,128]{2,1,0:T(8,128)S(1)}, f32[2,8,1024]{2,1,0:T(8,128)S(1)}, f32[8,128]{1,0:T(8,128)S(1)}, bf16[2,1024,512]{2,1,0:T(8,128)(2,1)S(1)}, bf16[2,1024,512]{2,1,0:T(8,128)(2,1)S(1)}) custom-call(f32[2,256,128]{2,1,0:T(8,128)S(1)} %bitcast.15, s32[1,512]{1,0:T(1,128)S(1)} %get-tuple-element.21.rows_ref, ...), custom_call_target="tpu_custom_call" | custom-call | tf_op jit(solution)/shard_map/degrees_there_and_back/pallas_call | solution.py:386
  52.9 21.0 %all_to_all.35 = f32[256,1,128]{2,1,0:T(1,128)S(1)} all-to-all(f32[256,1,128]{2,1,0:T(1,128)S(1)} %bitcast.19), channel_id=1, replica_groups=mesh['probe'=4,'place'=64,'core'=2] {'probe','place'}, dimensions={0} | all-to-all | bytes 262144 | tf_op jit(solution)/shard_map/all_to_all | solution.py:411
  73.9 3.3 %all-gather.1 = f32[512,1,128]{2,1,0:T(1,128)S(1)} all-gather(f32[256,1,128]{2,1,0:T(1,128)S(1)} %all_to_all.35), channel_id=3, replica_groups=mesh['probe'=4,'place'=64,'core'=2] {'core'}, dimensions={0}, use_global_device_ids=true | all-gather | bytes 393216 | tf_op jit(solution)/shard_map/all_gather | solution.py:414
  77.2 4.3 %cycles_there_and_back.1 = (f32[128,128]{1,0:T(8,128)S(1)}, f32[256,128]{1,0:T(8,128)S(1)}) custom-call(f32[2,256,128]{2,1,0:T(8,128)S(1)} %bitcast.16, s32[1,4,8192]{2,1,0:T(4,128)S(1)} %get-tuple-element.26.signs_ref, f32[4,8192]{1,0:T(4,128)S(1)} %get-tuple-element.27.inv_noise_ref, f32[256,128]{1,0:T(8,128)S(1)} %get-tuple-element.28.inner_cos_ref, ...), custom_call_target="tpu_custom_call" | custom-call | tf_op jit(solution)/shard_map/cycles_there_and_back/pallas_call | solution.py:386
  81.5 16.6 %all_to_all.36 = f32[128,1,128]{2,1,0:T(1,128)S(1)} all-to-all(f32[128,1,128]{2,1,0:T(1,128)S(1)} %bitcast.20), channel_id=1, replica_groups=mesh['probe'=4,'place'=64,'core'=2] {'place','core'}, dimensions={0} | all-to-all | bytes 131072 | tf_op jit(solution)/shard_map/all_to_all | solution.py:476
  98.1 1.7 %image_terms.1 = f32[4,328,128]{2,1,0:T(8,128)S(1)} custom-call(f32[128,128]{1,0:T(8,128)S(1)} %bitcast.17, s32[1,512]{1,0:T(1,128)S(1)} %get-tuple-element.21.rows_ref, f32[1,1024]{1,0:T(1,128)S(1)} %get-tuple-element.22.signal_ref, s32[8,128]{1,0:T(8,128)S(1)} %get-tuple-element.23.limits_ref, bf16[2,1024,512]{2,1,0:T(8,128)(2,1)S(1)} %get-tuple-element.34.hi_ref, ...), custom_call_target="tpu_custom_call" | custom-call | tf_op jit(solution)/shard_map/image_terms/pallas_call | solution.py:386
  99.8 12.4 %all_to_all.37.received_ref = f32[4,328,128]{2,1,0:T(8,128)S(1)} all-to-all(f32[4,328,128]{2,1,0:T(8,128)S(1)} %image_terms.1), channel_id=1, replica_groups=mesh['probe'=4,'place'=64,'core'=2] {'probe'}, dimensions={0} | all-to-all | bytes 1343488 | tf_op jit(solution)/shard_map/all_to_all | solution.py:485
  112.2 0.8 outputs.1
Async XLA Ops:
  0.6 2.2 %copy-start = (f32[2,1024,512]{2,1,0:T(8,128)S(1)}, f32[2,1024,512]{2,1,0:T(8,128)}, u32[]{:S(2)}) copy-start(f32[2,1024,512]{2,1,0:T(8,128)} %legendre_hbm.1) | copy-start | bytes 12582916
  2.8 0.9 copy-start.1
  3.7 0.9 copy-start.2
  4.6 0.7 copy-start.3
  5.3 0.7 copy-start.4
  6.0 0.7 copy-start.5

commit v3 on v2

--- a/solution.py
+++ b/solution.py
@@ -23,6 +23,10 @@
     return jnp.dot(a, b, preferred_element_type=F32)
 
 
+def dot_rows(a, b):
+    return lax.dot_general(a, b, (((1,), (1,)), ((), ())), preferred_element_type=F32)
+
+
 def halves(value):
     high = value.astype(BF16)
     return high, (value - high.astype(F32)).astype(BF16)
@@ -39,6 +43,11 @@
         folded_ref[j * cycles : (j + 1) * cycles, :] = flat_ref[
             :, j * LANES : (j + 1) * LANES
         ].astype(F32)
+
+
+def outer_sums(table_ref, hi, lo):
+    repeat = LANES // hi.shape[0]
+    return dot(table_ref[...], jnp.concatenate([hi, lo] * repeat, axis=0))
 
 
 def twiddle_sums(parts, inner_cos, inner_sin, acc, lane, base):
@@ -138,9 +147,7 @@
     pixels = jnp.concatenate(
         [folded_ref[pl.ds(f, outer, stride=cycles), :] for f in range(cycles)], axis=1
     ).astype(BF16)
-    parts = dot(outer_a_ref[:, :outer], pixels) + dot(
-        outer_a_ref[:, LANES : LANES + outer], pixels
-    )
+    parts = outer_sums(outer_a_ref, pixels, jnp.zeros_like(pixels))
     lane = iota((count, LANES), 1)
     acc = jnp.zeros((count, LANES), F32)
     rows = probes * 2
@@ -173,11 +180,12 @@
                 lane < width, high, jnp.where(lane < 2 * width, low, 0.0)
             )
     chosen = jnp.where(iota((total, total), 0) == rows_ref[...], 1.0, 0.0).astype(BF16)
-    return dot(chosen, stack_ref[...].astype(BF16)).astype(BF16), chosen
+    turned = stack_ref[...].T[: 2 * width].astype(BF16)
+    return dot_rows(turned, chosen).astype(BF16), chosen
 
 
 def degree_sums(leg_hi, leg_lo, columns, k, rows, width, order, first_degree):
-    across = (dot(leg_hi, columns) + dot(leg_lo, columns)).T
+    across = dot_rows(columns, leg_hi) + dot_rows(columns, leg_lo)
     terms = across[k * rows : (k + 1) * rows] + across[
         width + k * rows : width + (k + 1) * rows
     ]
@@ -191,7 +199,7 @@
 ):
     cores = received_ref.shape[0]
     probes, places = send_ref.shape[:2]
-    slots, quarter, total = legendre_ref.shape
+    slots, quarter, total = hi_ref.shape
     cycles = total // (places * cores)
     rows = probes * 2
     width = slots * rows
@@ -382,11 +390,16 @@
                 residual_ref[0, k, :, place : place + LANES] = residual[row : row + 2]
 
 
-def call(kernel, outs, scratch, args, name, space=pltpu.VMEM):
+def call(kernel, outs, scratch, args, name, far=()):
+    spaces = [pltpu.HBM if i in far else pltpu.VMEM for i in range(len(args))]
+    args = [
+        pltpu.with_memory_space_constraint(arg, space) if space == pltpu.HBM else arg
+        for arg, space in zip(args, spaces)
+    ]
     return pl.pallas_call(
         kernel,
         out_shape=[jax.ShapeDtypeStruct(shape, dtype) for shape, dtype in outs],
-        in_specs=[pl.BlockSpec(memory_space=space)] * len(args),
+        in_specs=[pl.BlockSpec(memory_space=space) for space in spaces],
         out_specs=[pl.BlockSpec(memory_space=pltpu.VMEM)] * len(outs),
         scratch_shapes=scratch,
         compiler_params=pltpu.CompilerParams(vmem_limit_bytes=VMEM_BYTES),
@@ -442,7 +455,7 @@
             inv_signal.reshape(1, probes * quarter), inv_noise, legendre,
         ),
         "cycle_sums",
-        pltpu.HBM,
+        range(6),
     )
     received = everywhere(send)
     send, terms, scalars, leg_hi, leg_lo = call(
@@ -454,7 +467,10 @@
             (legendre.shape, BF16),
             (legendre.shape, BF16),
         ],
-        [pltpu.VMEM(*wide), pltpu.VMEM(*wide)],
+        [
+            pltpu.VMEM(*wide),
+            pltpu.VMEM(*wide),
+        ],
         (received, row_line, signal, limits, legendre_near),
         "degrees_there_and_back",
     )

time: 114 us -> 106 us (0.930)
  local copies, waits for them, and re-layouts: 6.06 us -> 0 us
  Pallas kernels: 14.3 us -> 12.5 us
    unnamed x12 -> x0, local copies, waits for them, and re-layouts: 6.06 us -> none
    pallas_call x5, Pallas kernels: 14.3 us -> 12.5 us  [call(): pl.pallas_call(kernel, out_shape=[jax.ShapeDtypeStruct(shape, dtype) for...]
where the time goes in v3:
time: 106 us; the launch traced here: 105 us
  blocking collectives  92.1 us (87%)
  Pallas kernels  12.5 us (12%)
    all_to_all x2, blocking collectives, everywhere(): lax.all_to_all(send.reshape(probes * places, LANES), ('probe', 'place'),...  55.7 us
    all_to_all x1, blocking collectives, per_device(): received = lax.all_to_all(send, ('place', 'core'), 0, 0, tiled=True)  16.6 us
    pallas_call x5, Pallas kernels, call(): pl.pallas_call(kernel, out_shape=[jax.ShapeDtypeStruct(shape, dtype) for...  12.5 us
    all_to_all x1, blocking collectives, per_device(): received = lax.all_to_all(send, 'probe', 0, 0, tiled=True)  12.5 us
    all_gather x2, blocking collectives, everywhere(): return lax.all_gather(received, 'core', axis=0)  7.36 us

profile of v3, /device:TPU:1, one launch (start us, length us, event | category | flops | bytes accessed | tf_op | source)
XLA Modules:
  0.0 105.3 jit_solution(5759371476700718391)
XLA Ops:
  0.6 2.9 %cycle_sums.1 = (f32[4,64,128]{2,1,0:T(8,128)S(1)}, f32[256,128]{1,0:T(8,128)S(1)}, f32[256,128]{1,0:T(8,128)S(1)}, bf16[512,256]{1,0:T(8,128)(2,1)S(1)}, bf16[1...) custom-call(s32[1,256]{1,0:T(1,128)} %bitcast.23, ...), custom_call_target="tpu_custom_call" | custom-call | tf_op jit(solution)/shard_map/cycle_sums/pallas_call | solution.py:399
  3.6 34.9 %all_to_all.34 = f32[256,1,128]{2,1,0:T(1,128)S(1)} all-to-all(f32[256,1,128]{2,1,0:T(1,128)S(1)} %bitcast.18), channel_id=1, replica_groups=mesh['probe'=4,'place'=64,'core'=2] {'probe','place'}, dimensions={0} | all-to-all | bytes 262144 | tf_op jit(solution)/shard_map/all_to_all | solution.py:424
  38.4 3.9 %all-gather = f32[512,1,128]{2,1,0:T(1,128)S(1)} all-gather(f32[256,1,128]{2,1,0:T(1,128)S(1)} %all_to_all.34), channel_id=2, replica_groups=mesh['probe'=4,'place'=64,'core'=2] {'core'}, dimensions={0}, use_global_device_ids=true | all-gather | bytes 393216 | tf_op jit(solution)/shard_map/all_gather | solution.py:427
  42.3 2.9 %degrees_there_and_back.1 = (f32[4,64,128]{2,1,0:T(8,128)S(1)}, f32[2,8,1024]{2,1,0:T(8,128)S(1)}, f32[8,128]{1,0:T(8,128)S(1)}, bf16[2,1024,512]{2,1,0:T(8,128)(2,1)S(1)}, bf16[2,1024,512]{2,1,0:T(8,128)(2,1)S(1)}) custom-call(f32[2,256,128]{2,1,0:T(8,128)S(1)} %bitcast.15, s32[1,512]{1,0:T(1,128)S(1)} %get-tuple-element.21.rows_ref, ...), custom_call_target="tpu_custom_call" | custom-call | tf_op jit(solution)/shard_map/degrees_there_and_back/pallas_call | solution.py:399
  45.3 20.8 %all_to_all.35 = f32[256,1,128]{2,1,0:T(1,128)S(1)} all-to-all(f32[256,1,128]{2,1,0:T(1,128)S(1)} %bitcast.19), channel_id=1, replica_groups=mesh['probe'=4,'place'=64,'core'=2] {'probe','place'}, dimensions={0} | all-to-all | bytes 262144 | tf_op jit(solution)/shard_map/all_to_all | solution.py:424
  66.1 3.5 %all-gather.1 = f32[512,1,128]{2,1,0:T(1,128)S(1)} all-gather(f32[256,1,128]{2,1,0:T(1,128)S(1)} %all_to_all.35), channel_id=3, replica_groups=mesh['probe'=4,'place'=64,'core'=2] {'core'}, dimensions={0}, use_global_device_ids=true | all-gather | bytes 393216 | tf_op jit(solution)/shard_map/all_gather | solution.py:427
  69.5 4.2 %cycles_there_and_back.1 = (f32[128,128]{1,0:T(8,128)S(1)}, f32[256,128]{1,0:T(8,128)S(1)}) custom-call(f32[2,256,128]{2,1,0:T(8,128)S(1)} %bitcast.16, s32[1,4,8192]{2,1,0:T(4,128)S(1)} %get-tuple-element.26.signs_ref, f32[4,8192]{1,0:T(4,128)S(1)} %get-tuple-element.27.inv_noise_ref, f32[256,128]{1,0:T(8,128)S(1)} %get-tuple-element.28.inner_cos_ref, ...), custom_call_target="tpu_custom_call" | custom-call | tf_op jit(solution)/shard_map/cycles_there_and_back/pallas_call | solution.py:399
  73.8 16.6 %all_to_all.36 = f32[128,1,128]{2,1,0:T(1,128)S(1)} all-to-all(f32[128,1,128]{2,1,0:T(1,128)S(1)} %bitcast.20), channel_id=1, replica_groups=mesh['probe'=4,'place'=64,'core'=2] {'place','core'}, dimensions={0} | all-to-all | bytes 131072 | tf_op jit(solution)/shard_map/all_to_all | solution.py:492
  90.3 1.6 %image_terms.1 = f32[4,328,128]{2,1,0:T(8,128)S(1)} custom-call(f32[128,128]{1,0:T(8,128)S(1)} %bitcast.17, s32[1,512]{1,0:T(1,128)S(1)} %get-tuple-element.21.rows_ref, f32[1,1024]{1,0:T(1,128)S(1)} %get-tuple-element.22.signal_ref, s32[8,128]{1,0:T(8,128)S(1)} %get-tuple-element.23.limits_ref, bf16[2,1024,512]{2,1,0:T(8,128)(2,1)S(1)} %get-tuple-element.34.hi_ref, ...), custom_call_target="tpu_custom_call" | custom-call | tf_op jit(solution)/shard_map/image_terms/pallas_call | solution.py:399
  92.0 12.5 %all_to_all.37.received_ref = f32[4,328,128]{2,1,0:T(8,128)S(1)} all-to-all(f32[4,328,128]{2,1,0:T(8,128)S(1)} %image_terms.1), channel_id=1, replica_groups=mesh['probe'=4,'place'=64,'core'=2] {'probe'}, dimensions={0} | all-to-all | bytes 1343488 | tf_op jit(solution)/shard_map/all_to_all | solution.py:501
  104.5 0.8 outputs.1

commit v4 on v3

v4 whole, which is shorter than its diff:
```python
import functools
import math

import jax
import jax.numpy as jnp
from jax import lax
from jax.experimental import pallas as pl
from jax.experimental.pallas import tpu as pltpu
from jax.sharding import PartitionSpec as P

F32 = jnp.float32
BF16 = jnp.bfloat16
LANES = 128
VMEM_BYTES = 24 * 1024 * 1024


def iota(shape, dim):
    return lax.broadcasted_iota(jnp.int32, shape, dim)


def dot(a, b):
    return jnp.dot(a, b, preferred_element_type=F32)


def dot_rows(a, b):
    return lax.dot_general(a, b, (((1,), (1,)), ((), ())), preferred_element_type=F32)


def halves(value):
    high = value.astype(BF16)
    return high, (value - high.astype(F32)).astype(BF16)


def fold(flat_ref, f, copies):
    rows = [
        flat_ref[f : f + 1, j * LANES : (j + 1) * LANES] for j in range(flat_ref.shape[1] // LANES)
    ]
    return jnp.concatenate(rows * copies, axis=0)


def cosine(phase, turn):
    shift = turn.bit_length() - 3
    quadrant = (phase + turn // 8) >> shift
    angle = (phase - (quadrant << shift)).astype(F32) * (2.0 * math.pi / turn)
    square = angle * angle
    cos = 1.0 + square * (
        -1.0 / 2 + square * (1.0 / 24 + square * (-1.0 / 720 + square * (1.0 / 40320)))
    )
    sin = angle * (
        1.0 + square * (-1.0 / 6 + square * (1.0 / 120 + square * (-1.0 / 5040 + square / 362880)))
    )
    value = jnp.where((quadrant & 1) == 1, sin, cos)
    return jnp.where(((quadrant + 1) & 2) == 2, -value, value)


def cosine_and_sine(rows, step, turn):
    half = LANES // 2
    lane = iota((rows, LANES), 1)
    phase = iota((rows, LANES), 0) * (lane & (half - 1)) * step
    return cosine(phase - jnp.where(lane >= half, turn // 4, 0), turn)


def ones_where(condition):
    return jnp.where(condition, 1.0, 0.0).astype(BF16)


def both_picks(line):
    half = LANES // 2
    count = line.shape[1]
    shape = (LANES, 2 * count)
    row, col = iota(shape, 0), iota(shape, 1)
    wide = jnp.concatenate([line, line], axis=1)
    return ones_where(row == wide + jnp.where(col >= count, half, 0))


def turned_rows(pieces):
    rows = jnp.concatenate(pieces, axis=0)
    if rows.shape[0] < LANES:
        rows = jnp.concatenate(
            [rows, jnp.zeros((LANES - rows.shape[0], rows.shape[1]), F32)], axis=0
        )
    return rows.T


def own_rows(received_ref, source, groups):
    places = received_ref.shape[1] // groups
    total = received_ref[source, :places]
    for g in range(1, groups):
        total = total + received_ref[source, g * places : (g + 1) * places]
    total = total.T
    half = LANES // 2
    return jnp.where(lax.axis_index("core") == 0, total[:half], total[half:])


def first_kernel(
    slots, orders_hbm, signs_hbm, rows_hbm, signal_hbm, noise_hbm,
    send_ref, inner_cos_ref, inner_sin_ref, outer_ref, limits_ref, signs_ref,
    rows_ref, signal_ref, noise_ref,
    orders_ref, near_rows_ref, sems,
):
    count = orders_ref.shape[1]
    probes, places = send_ref.shape[:2]
    _, cycles, cycle_length = signs_ref.shape
    outer = cycle_length // LANES
    cores = count // slots // places
    total = rows_ref.shape[1]
    own = lax.axis_index("probe")
    quarter = signal_ref.shape[1]
    own_signal = signal_hbm.at[:, pl.ds(pl.multiple_of(own * quarter, LANES), quarter)]

    copies = [
        pltpu.make_async_copy(source, target, sems.at[n])
        for n, (source, target) in enumerate(
            [
                (orders_hbm, orders_ref),
                (signs_hbm, signs_ref),
                (rows_hbm, near_rows_ref),
                (own_signal, signal_ref),
                (noise_hbm, noise_ref),
            ]
        )
    ]
    for copy in copies:
        copy.start()

    high_table = halves(cosine_and_sine(LANES, 64, cycle_length))
    low_table = halves(cosine_and_sine(LANES, 1, cycle_length))
    outer_table = halves(cosine_and_sine(outer, cycle_length // outer, cycle_length))
    slot, place = iota((count, count), 0), iota((count, count), 1)
    slot_picks = ones_where(
        slot == (place % places * cores + place // places % cores) * slots
        + place // (places * cores)
    )

    copies[0].wait()
    orders = orders_ref[...]
    row = iota((8, count), 0)
    parts = jnp.where(row == 0, orders >> 6, jnp.where(row == 1, orders & 63, 0))
    parts = dot(parts.astype(F32).astype(BF16), slot_picks).astype(jnp.int32)
    high, low = parts[:1], parts[1:2]
    for k in range(slots):
        own_place = (k * cores + lax.axis_index("core")) * places + lax.axis_index("place")
        picked = jnp.where(iota((1, count), 1) == own_place, high * 64 + low, 0).astype(F32)
        picked = jnp.sum(picked, axis=1, keepdims=True).astype(jnp.int32)
        limits_ref[k : k + 1, :] = jnp.broadcast_to(picked, (1, LANES))
    high_picks, low_picks = both_picks(high), both_picks(low)
    high_part = dot(high_table[0], high_picks) + dot(high_table[1], high_picks)
    low_part = dot(low_table[0], low_picks) + dot(low_table[1], low_picks)
    scale_factor = 1.0 / math.sqrt(cycle_length)
    high_cos, high_sin = high_part[:, :count] * scale_factor, high_part[:, count:] * scale_factor
    low_cos, low_sin = low_part[:, :count], low_part[:, count:]
    inner_cos = high_cos * low_cos - high_sin * low_sin
    inner_sin = high_sin * low_cos + high_cos * low_sin
    inner_cos_ref[...] = inner_cos
    inner_sin_ref[...] = inner_sin
    for h in range(2):
        table = dot(outer_table[h], low_picks).astype(BF16)
        outer_ref[2 * h * outer : (2 * h + 1) * outer, :] = table
        outer_ref[(2 * h + 1) * outer : (2 * h + 2) * outer, :] = table

    copies[1].wait()
    rows = probes * 2
    row = iota((rows, count), 0)
    pixels = jnp.concatenate(
        [fold(signs_ref.at[0], f, 2).astype(F32).T for f in range(cycles)], axis=0
    ).astype(BF16)
    sums = dot(pixels, outer_ref[outer : 3 * outer, :])
    pieces = [[None] * cycles for _ in range(slots)]
    per_slot = count // slots
    for f in range(cycles):
        cos_sum, sin_sum = twiddle_sums(sums[f * LANES : (f + 1) * LANES], inner_cos, inner_sin)
        field = jnp.where(
            row == own * 2, cos_sum, jnp.where(row == own * 2 + 1, sin_sum, 0.0)
        )
        for k in range(slots):
            pieces[k][f] = field[:, k * per_slot : (k + 1) * per_slot]
    out = turned_rows(
        [
            pieces[k][f][:, c * places : (c + 1) * places]
            for c in range(cores)
            for k in range(slots)
            for f in range(cycles)
        ]
    )
    for p in range(probes):
        send_ref[p] = out

    for copy in copies[2:]:
        copy.wait()
    cycle_rows = near_rows_ref[...]
    row = iota((8, total), 0)
    parts = jnp.where(row == 0, cycle_rows >> 6, jnp.where(row == 1, cycle_rows & 63, 0))
    cycle, place = iota((total, total), 0), iota((total, total), 1)
    picks = ones_where(
        cycle == (place % places * cores + place // (places * cycles)) * cycles
        + place // places % cycles
    )
    parts = dot(parts.astype(F32).astype(BF16), picks).astype(jnp.int32)
    rows_ref[...] = parts[:1] * 64 + parts[1:2]


def twiddle_sums(sums, inner_cos, inner_sin):
    count = inner_cos.shape[1]
    real, imag = sums[:, :count], sums[:, count:]
    return (
        jnp.sum(inner_cos * real - inner_sin * imag, axis=0, keepdims=True),
        jnp.sum(inner_sin * real + inner_cos * imag, axis=0, keepdims=True),
    )


def latitude_values(by_core, chosen, slots, cycles, rows):
    values = [
        jnp.concatenate(
            [
                values[(k * cycles + f) * rows : (k * cycles + f + 1) * rows]
                for values in by_core
                for f in range(cycles)
            ],
            axis=1,
        )
        for k in range(slots)
    ]
    both = jnp.concatenate(halves(jnp.concatenate(values, axis=0)), axis=0)
    return dot_rows(both, chosen).astype(BF16)


def degree_sums(leg_hi, leg_lo, values, k, rows, order, first_degree):
    width = values.shape[0] // 2
    across = dot_rows(values, leg_hi) + dot_rows(values, leg_lo)
    terms = across[k * rows : (k + 1) * rows] + across[
        width + k * rows : width + (k + 1) * rows
    ]
    degrees = first_degree + iota(terms.shape, 1)
    return jnp.where(degrees >= order, terms, 0.0)


def second_kernel(
    received_ref, rows_ref, signal_ref, limits_ref, legendre_ref,
    send_ref, terms_ref, scalars_ref, hi_ref, lo_ref, chosen_ref,
):
    cores = received_ref.shape[0]
    probes, places = send_ref.shape[:2]
    slots, quarter, total = legendre_ref.shape
    cycles = total // (places * cores)
    rows = probes * 2
    width = slots * rows
    chosen = ones_where(iota((total, total), 0) == rows_ref[...])
    chosen_ref[...] = chosen
    values = latitude_values(
        [own_rows(received_ref, c, probes) for c in range(cores)], chosen, slots, cycles, rows
    )
    first_degree = lax.axis_index("probe") * quarter
    signal = signal_ref[...]
    norm = jnp.zeros((rows, 1), F32)
    prior = jnp.zeros((rows, 1), F32)
    halved = []
    for k in range(slots):
        leg_hi, leg_lo = halves(legendre_ref[k])
        hi_ref[k] = leg_hi
        lo_ref[k] = leg_lo
        halved.append((leg_hi, leg_lo))
    both = []
    for k in range(slots):
        terms = degree_sums(
            *halved[k], values, k, rows, limits_ref[k : k + 1, :1], first_degree
        )
        terms_ref[k] = terms
        squares = terms * terms
        norm = norm + jnp.sum(squares, axis=1, keepdims=True)
        prior = prior + jnp.sum(squares * signal, axis=1, keepdims=True)
        both.append(jnp.concatenate(halves(terms), axis=0))
    fields = []
    for k in range(slots):
        field = dot(both[k], halved[k][0]) + dot(both[k], halved[k][1])
        fields.append(field[:rows] + field[rows:])
    both = jnp.concatenate(halves(jnp.concatenate(fields, axis=0)), axis=0)
    by_cycle = dot(both, chosen)
    by_cycle = by_cycle[:width] + by_cycle[width:]
    out = turned_rows(
        [
            by_cycle[k * rows : (k + 1) * rows, place * places : (place + 1) * places]
            for c in range(cores)
            for k in range(slots)
            for place in range(c * cycles, (c + 1) * cycles)
        ]
    )
    for p in range(probes):
        send_ref[p] = out
    scalars_ref[:rows, :] = jnp.broadcast_to(norm, (rows, LANES))
    scalars_ref[rows:, :] = jnp.broadcast_to(prior, (rows, LANES))


def third_kernel(
    slots, received_ref, signs_ref, inv_noise_ref, inner_cos_ref, inner_sin_ref, outer_ref,
    scalars_ref, send_ref, weighted_ref, mapped_ref,
):
    cores = received_ref.shape[0]
    places = send_ref.shape[0] // cores
    probes = received_ref.shape[1] // places
    cycles = inv_noise_ref.shape[0]
    outer = outer_ref.shape[0] // 4
    rows = probes * 2
    own = lax.axis_index("probe")

    by_core = [own_rows(received_ref, c, probes) for c in range(cores)]
    inner_cos, inner_sin = inner_cos_ref[...], inner_sin_ref[...]
    count = inner_cos.shape[1]
    per_slot = count // slots
    row = iota((rows, count), 0)
    power = jnp.zeros((rows, LANES), F32)
    power_row = iota((rows, LANES), 0)
    pieces = [[None] * cycles for _ in range(slots)]
    table = outer_ref[outer : 3 * outer, :]

    def map_cycle(f):
        coeffs = jnp.concatenate(
            [
                by_core[c][(k * cycles + f) * rows : (k * cycles + f + 1) * rows]
                for k in range(slots)
                for c in range(cores)
            ],
            axis=1,
        )
        fields = []
        for p in range(probes):
            cos_coeff, sin_coeff = coeffs[2 * p : 2 * p + 1], coeffs[2 * p + 1 : 2 * p + 2]
            real = cos_coeff * inner_cos + sin_coeff * inner_sin
            imag = sin_coeff * inner_cos - cos_coeff * inner_sin
            hi, lo = halves(jnp.concatenate([real, imag], axis=1))
            fields.append(dot_rows(hi, table) + dot_rows(lo, table))
        mapped = jnp.concatenate(fields, axis=0)
        return mapped + pltpu.roll(mapped, outer, 1)

    def weigh_cycle(f, mapped):
        mapped_ref[f] = mapped
        noise = fold(inv_noise_ref, f, 2).T
        pixels = jnp.concatenate([noise] * probes, axis=0) * mapped
        squares = pixels * mapped
        lines = [
            jnp.sum(squares[p * LANES : (p + 1) * LANES], axis=0, keepdims=True)
            for p in range(probes)
        ]
        hi = pixels.astype(BF16).astype(F32)
        hi_lo = jnp.where(iota(pixels.shape, 1) < outer, hi, pixels - hi).astype(BF16)
        return lines, outer_sums(hi_lo)

    def outer_sums(hi_lo):
        sums = dot(jnp.concatenate([hi_lo, hi_lo], axis=1), outer_ref[...])
        return [sums[p * LANES : (p + 1) * LANES] for p in range(probes)]

    def finish_cycle(f, lines, sums):
        nonlocal power
        field = jnp.zeros((rows, count), F32)
        for p in range(probes):
            power = power + jnp.where(power_row == 2 * p, lines[p], 0.0)
            cos_sum, sin_sum = twiddle_sums(sums[p], inner_cos, inner_sin)
            field = jnp.where(row == 2 * p, cos_sum, field)
            field = jnp.where(row == 2 * p + 1, sin_sum, field)
        for k in range(slots):
            pieces[k][f] = field[:, k * per_slot : (k + 1) * per_slot]

    mapped, done = map_cycle(0), None
    for f in range(cycles):
        later = map_cycle(f + 1) if f + 1 < cycles else None
        lines, sums = weigh_cycle(f, mapped)
        if done:
            finish_cycle(*done)
        mapped, done = later, (f, lines, sums)
    finish_cycle(*done)
    for f in range(cycles):
        picked = mapped_ref[f, pl.ds(pl.multiple_of(own * LANES, LANES), LANES), :].T
        weighted_ref[pl.ds(f, outer, stride=cycles), :] = picked[:outer] * fold(
            signs_ref.at[0], f, 1
        ).astype(F32)
    power = jnp.broadcast_to(0.5 * jnp.sum(power, axis=1, keepdims=True), (rows, per_slot))
    out = turned_rows(
        [pieces[k][f] for k in range(slots) for f in range(cycles)]
        + [scalars_ref[:, :per_slot], power]
    )
    for c in range(cores):
        send_ref[pl.ds(c, places, stride=cores), :] = out[c * places : (c + 1) * places]


def fourth_kernel(
    cores, received_ref, signal_ref, limits_ref, hi_ref, lo_ref, chosen_ref, terms_ref,
    weighted_ref, send_ref,
):
    probes = send_ref.shape[0]
    slots, quarter, total = hi_ref.shape
    cycles = total // received_ref.shape[0]
    places = received_ref.shape[0] // cores
    rows = probes * 2
    blocks = quarter // LANES
    block_rows = blocks * slots * 2
    by_core = [received_ref[pl.ds(c, places, stride=cores), :].T for c in range(cores)]
    start = slots * cycles * rows
    scalars = jnp.sum(by_core[0][start : start + 3 * rows], axis=1, keepdims=True)
    for values in by_core[1:]:
        scalars = scalars + jnp.sum(values[start : start + 3 * rows], axis=1, keepdims=True)
    scalars = jnp.broadcast_to(scalars, (3 * rows, LANES))
    for p in range(probes):
        send_ref[p, 2 * block_rows : 2 * block_rows + 3 * rows, :] = scalars
        send_ref[p, 2 * block_rows + 3 * rows :, :] = weighted_ref[...]
    values = latitude_values(by_core, chosen_ref[...], slots, cycles, rows)
    first_degree = lax.axis_index("probe") * quarter
    signal = signal_ref[...]
    for k in range(slots):
        noise_terms = degree_sums(
            hi_ref[k], lo_ref[k], values, k, rows, limits_ref[k : k + 1, :1], first_degree
        )
        terms = terms_ref[k]
        image = signal * terms + noise_terms
        for p in range(probes):
            for b in range(blocks):
                place = (b * slots + k) * 2
                own = (slice(p * 2, p * 2 + 2), slice(b * LANES, (b + 1) * LANES))
                send_ref[p, place : place + 2, :] = terms[own]
                send_ref[p, block_rows + place : block_rows + place + 2, :] = image[own]


def last_kernel(received_ref, residual_ref, variance_ref):
    probes = received_ref.shape[0]
    slots = residual_ref.shape[1]
    quarter = residual_ref.shape[3] // probes
    blocks = quarter // LANES
    block_rows = blocks * slots * 2
    rows = probes * 2
    cycles, length = variance_ref.shape
    own = lax.axis_index("probe")
    start = 2 * block_rows
    degree_sums = received_ref[0, start : start + 2 * rows, :]
    for p in range(1, probes):
        degree_sums = degree_sums + received_ref[p, start : start + 2 * rows, :]
    norm, prior = degree_sums[:rows], degree_sums[rows:]
    curve = prior + received_ref[0, start + 2 * rows : start + 3 * rows, :]
    ratios = [
        (norm[2 * p : 2 * p + 1] + norm[2 * p + 1 : 2 * p + 2])
        / (curve[2 * p : 2 * p + 1] + curve[2 * p + 1 : 2 * p + 2])
        for p in range(probes)
    ]
    start = start + 3 * rows
    total = received_ref[0, start:, :] * ratios[0]
    for p in range(1, probes):
        total = total + received_ref[p, start:, :] * ratios[p]
    total = total * (1.0 / probes)
    for j in range(length // LANES):
        variance_ref[:, j * LANES : (j + 1) * LANES] = total[j * cycles : (j + 1) * cycles]
    own_ratio = ratios[0]
    for p in range(1, probes):
        own_ratio = jnp.where(own == p, ratios[p], own_ratio)
    for x in range(probes):
        residual = (
            received_ref[x, :block_rows, :]
            - own_ratio * received_ref[x, block_rows : 2 * block_rows, :]
        )
        for b in range(blocks):
            for k in range(slots):
                place = x * quarter + b * LANES
                row = (b * slots + k) * 2
                residual_ref[0, k, :, place : place + LANES] = residual[row : row + 2]


def call(kernel, outs, scratch, args, name, far=()):
    spaces = [pltpu.HBM if i in far else pltpu.VMEM for i in range(len(args))]
    args = [
        pltpu.with_memory_space_constraint(arg, space) if space == pltpu.HBM else arg
        for arg, space in zip(args, spaces)
    ]
    return pl.pallas_call(
        kernel,
        out_shape=[jax.ShapeDtypeStruct(shape, dtype) for shape, dtype in outs],
        in_specs=[pl.BlockSpec(memory_space=space) for space in spaces],
        out_specs=[pl.BlockSpec(memory_space=pltpu.VMEM)] * len(outs),
        scratch_shapes=scratch,
        compiler_params=pltpu.CompilerParams(vmem_limit_bytes=VMEM_BYTES),
        name=name,
        cost_estimate=pl.CostEstimate(flops=2000000000, bytes_accessed=20000000, transcendentals=0),
    )(*args)


def per_device(legendre, signs, inv_noise, inv_signal, harmonic_order_values, cycle_rows):
    slots, quarter, total = legendre.shape
    _, cycles, length = signs.shape
    probes = lax.axis_size("probe")
    places = lax.axis_size("place")
    cores = lax.axis_size("core")
    count = harmonic_order_values.shape[0]
    outer = length // LANES
    rows = probes * 2
    by_order = ((LANES, count), F32)
    folded = ((outer * cycles, LANES), F32)

    def everywhere(send):
        received = lax.all_to_all(
            send.reshape(probes * places, LANES), ("probe", "place"), 0, 0, tiled=True
        )
        return lax.all_gather(received, "core", axis=0)

    (
        send, inner_cos, inner_sin, outer_table, limits, signs_near, row_line, signal,
        noise_near,
    ) = call(
        functools.partial(first_kernel, slots),
        [
            ((probes, places, LANES), F32),
            by_order,
            by_order,
            ((4 * outer, 2 * count), BF16),
            ((8, LANES), jnp.int32),
            (signs.shape, jnp.int32),
            ((1, total), jnp.int32),
            ((1, quarter), F32),
            (inv_noise.shape, F32),
        ],
        [
            pltpu.VMEM((1, count), jnp.int32),
            pltpu.VMEM((1, total), jnp.int32),
            pltpu.SemaphoreType.DMA((5,)),
        ],
        (
            harmonic_order_values.reshape(1, count), signs, cycle_rows.reshape(1, total),
            inv_signal.reshape(1, probes * quarter), inv_noise,
        ),
        "cycle_sums",
        range(5),
    )
    received = everywhere(send)
    send, terms, scalars, leg_hi, leg_lo, chosen = call(
        second_kernel,
        [
            ((probes, places, LANES), F32),
            ((slots, rows, quarter), F32),
            ((2 * rows, LANES), F32),
            (legendre.shape, BF16),
            (legendre.shape, BF16),
            ((total, total), BF16),
        ],
        [],
        (received, row_line, signal, limits, legendre),
        "degrees_there_and_back",
    )
    received = everywhere(send)
    send, weighted = call(
        functools.partial(third_kernel, slots),
        [((places * cores, LANES), F32), folded],
        [pltpu.VMEM((cycles, probes * LANES, LANES), F32)],
        (received, signs_near, noise_near, inner_cos, inner_sin, outer_table, scalars),
        "cycles_there_and_back",
    )
    received = lax.all_to_all(send, ("place", "core"), 0, 0, tiled=True)
    height = quarter // LANES * slots * 4 + 3 * rows + outer * cycles
    (send,) = call(
        functools.partial(fourth_kernel, cores),
        [((probes, height, LANES), F32)],
        [],
        (received, signal, limits, leg_hi, leg_lo, chosen, terms, weighted),
        "image_terms",
    )
    received = lax.all_to_all(send, "probe", 0, 0, tiled=True)
    return call(
        last_kernel,
        [((1, slots, 2, probes * quarter), F32), ((cycles, length), F32)],
        [],
        (received,),
        "outputs",
    )


def solution(mesh):
    cores = 2
    split = jax.sharding.Mesh(
        mesh.devices.reshape(mesh.shape["probe"], -1, cores), ("probe", "place", "core")
    )
    sky = ("place", "core")
    in_specs = (P(sky, "probe", None), P("probe", sky, None), P(sky, None), P(), P(), P())
    out_specs = (P("probe", sky, None, None), P(sky, None))

    def run(*args):
        return tuple(
            jax.shard_map(
                per_device, mesh=split, in_specs=in_specs, out_specs=out_specs, check_vma=False
            )(*args)
        )

    return run
```

time: 106 us -> 103 us (0.972)
  Pallas kernels: 12.5 us -> 9.63 us
    pallas_call x5, Pallas kernels: 12.5 us -> 9.63 us  [call(): pl.pallas_call(kernel, out_shape=[jax.ShapeDtypeStruct(shape, dtype) for...]
where the time goes in v4:
time: 103 us
  blocking collectives  92.7 us (90%)
  Pallas kernels  9.63 us (9%)
    all_to_all x2, blocking collectives, everywhere(): lax.all_to_all(send.reshape(probes * places, LANES), ('probe', 'place'),...  55.7 us
    all_to_all x1, blocking collectives, per_device(): received = lax.all_to_all(send, ('place', 'core'), 0, 0, tiled=True)  16.6 us
    all_to_all x1, blocking collectives, per_device(): received = lax.all_to_all(send, 'probe', 0, 0, tiled=True)  13.2 us
    pallas_call x5, Pallas kernels, call(): pl.pallas_call(kernel, out_shape=[jax.ShapeDtypeStruct(shape, dtype) for...  9.63 us
    all_gather x2, blocking collectives, everywhere(): return lax.all_gather(received, 'core', axis=0)  7.35 us

profile of v4, /device:TPU:1, one launch (start us, length us, event | category | flops | bytes accessed | tf_op | source)
XLA Modules:
  0.0 103.0 jit_solution(11004803511237992472)
XLA Ops:
  0.6 0.0 copy-start
  0.6 2.1 %cycle_sums.1 = (f32[4,64,128]{2,1,0:T(8,128)S(1)}, f32[128,256]{1,0:T(8,128)S(1)}, f32[128,256]{1,0:T(8,128)S(1)}, bf16[256,512]{1,0:T(8,128)(2,1)S(1)}, s32[8,...) custom-call(s32[1,256]{1,0:T(1,128)} %bitcast.23, ...), custom_call_target="tpu_custom_call" | custom-call | flops 2000000000 | bytes 20000000 | tf_op jit(solution)/shard_map/cycle_sums/pallas_call | solution.py:469
  2.7 34.8 %all_to_all.34 = f32[256,1,128]{2,1,0:T(1,128)S(1)} all-to-all(f32[256,1,128]{2,1,0:T(1,128)S(1)} %bitcast.17), channel_id=1, replica_groups=mesh['probe'=4,'place'=64,'core'=2] {'probe','place'}, dimensions={0} | all-to-all | bytes 262144 | tf_op jit(solution)/shard_map/all_to_all | solution.py:494
  37.6 3.9 %all-gather = f32[512,1,128]{2,1,0:T(1,128)S(1)} all-gather(f32[256,1,128]{2,1,0:T(1,128)S(1)} %all_to_all.34), channel_id=2, replica_groups=mesh['probe'=4,'place'=64,'core'=2] {'core'}, dimensions={0}, use_global_device_ids=true | all-gather | bytes 393216 | tf_op jit(solution)/shard_map/all_gather | solution.py:497
  41.5 0.0 copy-done
  41.5 2.7 %degrees_there_and_back.1 = (f32[4,64,128]{2,1,0:T(8,128)S(1)}, f32[2,8,1024]{2,1,0:T(8,128)S(1)}, f32[16,128]{1,0:T(8,128)S(1)}, bf16[2,1024,512]{2,1,0:T(8,128...) custom-call(f32[2,256,128]{2,1,0:T(8,128)S(1)} %bitcast.16, ...), custom_call_target="tpu_custom_call" | custom-call | flops 2000000000 | bytes 20000000 | tf_op jit(solution)/shard_map/degrees_there_and_back/pallas_call | solution.py:469
  44.1 20.8 %all_to_all.35 = f32[256,1,128]{2,1,0:T(1,128)S(1)} all-to-all(f32[256,1,128]{2,1,0:T(1,128)S(1)} %bitcast.18), channel_id=1, replica_groups=mesh['probe'=4,'place'=64,'core'=2] {'probe','place'}, dimensions={0} | all-to-all | bytes 262144 | tf_op jit(solution)/shard_map/all_to_all | solution.py:494
  65.0 3.5 %all-gather.1 = f32[512,1,128]{2,1,0:T(1,128)S(1)} all-gather(f32[256,1,128]{2,1,0:T(1,128)S(1)} %all_to_all.35), channel_id=3, replica_groups=mesh['probe'=4,'place'=64,'core'=2] {'core'}, dimensions={0}, use_global_device_ids=true | all-gather | bytes 393216 | tf_op jit(solution)/shard_map/all_gather | solution.py:497
  68.4 2.7 %cycles_there_and_back.1 = (f32[128,128]{1,0:T(8,128)S(1)}, f32[256,128]{1,0:T(8,128)S(1)}) custom-call(f32[2,256,128]{2,1,0:T(8,128)S(1)} %bitcast.15, s32[1,4,8192]{2,1,0:T(4,128)S(1)} %get-tuple-element.24.signs_ref, f32[4,8192]{1,0:T(4,128)S(1)} %get-tuple-element.25.inv_noise_ref, f32[128,256]{1,0:T(8,128)S(1)} %get-tuple-element.26.inner_cos_ref, ...), custom_call_target="tpu_custom_call" | custom-call | flops 2000000000 | bytes 20000000 | tf_op jit(solution)/shard_map/cycles_there_and_back/pallas_call | solution.py:469
  71.1 16.6 %all_to_all.36 = f32[128,1,128]{2,1,0:T(1,128)S(1)} all-to-all(f32[128,1,128]{2,1,0:T(1,128)S(1)} %bitcast.20), channel_id=1, replica_groups=mesh['probe'=4,'place'=64,'core'=2] {'place','core'}, dimensions={0} | all-to-all | bytes 131072 | tf_op jit(solution)/shard_map/all_to_all | solution.py:550
  87.6 1.5 %image_terms.1 = f32[4,344,128]{2,1,0:T(8,128)S(1)} custom-call(f32[128,128]{1,0:T(8,128)S(1)} %bitcast.19, f32[1,1024]{1,0:T(1,128)S(1)} %get-tuple-element.21.signal_ref, s32[8,128]{1,0:T(8,128)S(1)} %get-tuple-element.22.limits_ref, bf16[2,1024,512]{2,1,0:T(8,128)(2,1)S(1)} %get-tuple-element.31.hi_ref, ...), custom_call_target="tpu_custom_call" | custom-call | flops 2000000000 | bytes 20000000 | tf_op jit(solution)/shard_map/image_terms/pallas_call | solution.py:469
  89.2 13.2 %all_to_all.37.received_ref = f32[4,344,128]{2,1,0:T(8,128)S(1)} all-to-all(f32[4,344,128]{2,1,0:T(8,128)S(1)} %image_terms.1), channel_id=1, replica_groups=mesh['probe'=4,'place'=64,'core'=2] {'probe'}, dimensions={0} | all-to-all | bytes 1409024 | tf_op jit(solution)/shard_map/all_to_all | solution.py:559
  102.3 0.7 outputs.1
Async XLA Ops:
  0.6 40.8 %copy-start = (f32[2,1024,512]{2,1,0:T(8,128)S(1)}, f32[2,1024,512]{2,1,0:T(8,128)}, u32[]{:S(2)}) copy-start(f32[2,1024,512]{2,1,0:T(8,128)} %legendre_ref.1) | copy-start | bytes 12582916

commit v5 on v4

--- a/solution.py
+++ b/solution.py
@@ -31,11 +31,14 @@
     return high, (value - high.astype(F32)).astype(BF16)
 
 
-def fold(flat_ref, f, copies):
-    rows = [
-        flat_ref[f : f + 1, j * LANES : (j + 1) * LANES] for j in range(flat_ref.shape[1] // LANES)
-    ]
-    return jnp.concatenate(rows * copies, axis=0)
+def fold(flat_ref, f):
+    return jnp.concatenate(
+        [
+            flat_ref[f : f + 1, j * LANES : (j + 1) * LANES]
+            for j in range(flat_ref.shape[1] // LANES)
+        ],
+        axis=0,
+    )
 
 
 def cosine(phase, turn):
@@ -94,7 +97,7 @@
 
 def first_kernel(
     slots, orders_hbm, signs_hbm, rows_hbm, signal_hbm, noise_hbm,
-    send_ref, inner_cos_ref, inner_sin_ref, outer_ref, limits_ref, signs_ref,
+    send_ref, inner_ref, outer_ref, limits_ref, signs_ref,
     rows_ref, signal_ref, noise_ref,
     orders_ref, near_rows_ref, sems,
 ):
@@ -151,24 +154,23 @@
     low_cos, low_sin = low_part[:, :count], low_part[:, count:]
     inner_cos = high_cos * low_cos - high_sin * low_sin
     inner_sin = high_sin * low_cos + high_cos * low_sin
-    inner_cos_ref[...] = inner_cos
-    inner_sin_ref[...] = inner_sin
-    for h in range(2):
-        table = dot(outer_table[h], low_picks).astype(BF16)
-        outer_ref[2 * h * outer : (2 * h + 1) * outer, :] = table
-        outer_ref[(2 * h + 1) * outer : (2 * h + 2) * outer, :] = table
+    inner = halves(jnp.concatenate([inner_cos, inner_sin], axis=1))
+    for n in range(4):
+        inner_ref[n * LANES : (n + 1) * LANES, :] = inner[n // 2]
+    outer_part = dot(outer_table[0], low_picks) + dot(outer_table[1], low_picks)
+    outer_ref[...] = outer_part
 
     copies[1].wait()
     rows = probes * 2
     row = iota((rows, count), 0)
     pixels = jnp.concatenate(
-        [fold(signs_ref.at[0], f, 2).astype(F32).T for f in range(cycles)], axis=0
+        [fold(signs_ref.at[0], f).astype(F32) for f in range(cycles)], axis=0
     ).astype(BF16)
-    sums = dot(pixels, outer_ref[outer : 3 * outer, :])
+    sums = dot(jnp.concatenate([pixels, pixels], axis=1), inner_ref[LANES : 3 * LANES, :])
     pieces = [[None] * cycles for _ in range(slots)]
     per_slot = count // slots
     for f in range(cycles):
-        cos_sum, sin_sum = twiddle_sums(sums[f * LANES : (f + 1) * LANES], inner_cos, inner_sin)
+        cos_sum, sin_sum = twiddle_sums(sums[f * outer : (f + 1) * outer], outer_part)
         field = jnp.where(
             row == own * 2, cos_sum, jnp.where(row == own * 2 + 1, sin_sum, 0.0)
         )
@@ -199,12 +201,13 @@
     rows_ref[...] = parts[:1] * 64 + parts[1:2]
 
 
-def twiddle_sums(sums, inner_cos, inner_sin):
-    count = inner_cos.shape[1]
-    real, imag = sums[:, :count], sums[:, count:]
+def twiddle_sums(sums, table):
+    count = table.shape[1] // 2
+    cos, sin = table[:, :count], table[:, count:]
+    by_cos, by_sin = sums[:, :count], sums[:, count:]
     return (
-        jnp.sum(inner_cos * real - inner_sin * imag, axis=0, keepdims=True),
-        jnp.sum(inner_sin * real + inner_cos * imag, axis=0, keepdims=True),
+        jnp.sum(cos * by_cos - sin * by_sin, axis=0, keepdims=True),
+        jnp.sum(sin * by_cos + cos * by_sin, axis=0, keepdims=True),
     )
 
 
@@ -291,26 +294,25 @@
 
 
 def third_kernel(
-    slots, received_ref, signs_ref, inv_noise_ref, inner_cos_ref, inner_sin_ref, outer_ref,
-    scalars_ref, send_ref, weighted_ref, mapped_ref,
+    slots, received_ref, signs_ref, inv_noise_ref, inner_ref, outer_ref, scalars_ref,
+    send_ref, weighted_ref, mapped_ref,
 ):
     cores = received_ref.shape[0]
     places = send_ref.shape[0] // cores
     probes = received_ref.shape[1] // places
     cycles = inv_noise_ref.shape[0]
-    outer = outer_ref.shape[0] // 4
+    outer, count = outer_ref.shape[0], outer_ref.shape[1] // 2
     rows = probes * 2
     own = lax.axis_index("probe")
 
     by_core = [own_rows(received_ref, c, probes) for c in range(cores)]
-    inner_cos, inner_sin = inner_cos_ref[...], inner_sin_ref[...]
-    count = inner_cos.shape[1]
+    outer_cos, outer_sin = outer_ref[:, :count], outer_ref[:, count:]
     per_slot = count // slots
     row = iota((rows, count), 0)
     power = jnp.zeros((rows, LANES), F32)
     power_row = iota((rows, LANES), 0)
     pieces = [[None] * cycles for _ in range(slots)]
-    table = outer_ref[outer : 3 * outer, :]
+    table = inner_ref[LANES : 3 * LANES, :]
 
     def map_cycle(f):
         coeffs = jnp.concatenate(
@@ -321,39 +323,37 @@
             ],
             axis=1,
         )
-        fields = []
+        high, low = [], []
         for p in range(probes):
             cos_coeff, sin_coeff = coeffs[2 * p : 2 * p + 1], coeffs[2 * p + 1 : 2 * p + 2]
-            real = cos_coeff * inner_cos + sin_coeff * inner_sin
-            imag = sin_coeff * inner_cos - cos_coeff * inner_sin
-            hi, lo = halves(jnp.concatenate([real, imag], axis=1))
-            fields.append(dot_rows(hi, table) + dot_rows(lo, table))
-        mapped = jnp.concatenate(fields, axis=0)
-        return mapped + pltpu.roll(mapped, outer, 1)
+            by_cos = cos_coeff * outer_cos + sin_coeff * outer_sin
+            by_sin = sin_coeff * outer_cos - cos_coeff * outer_sin
+            hi, lo = halves(jnp.concatenate([by_cos, by_sin], axis=1))
+            high.append(hi)
+            low.append(lo)
+        mapped = dot_rows(jnp.concatenate(high, axis=0), table) + dot_rows(
+            jnp.concatenate(low, axis=0), table
+        )
+        return mapped[:, :LANES] + mapped[:, LANES:]
 
     def weigh_cycle(f, mapped):
         mapped_ref[f] = mapped
-        noise = fold(inv_noise_ref, f, 2).T
-        pixels = jnp.concatenate([noise] * probes, axis=0) * mapped
+        pixels = jnp.concatenate([fold(inv_noise_ref, f)] * probes, axis=0) * mapped
         squares = pixels * mapped
         lines = [
-            jnp.sum(squares[p * LANES : (p + 1) * LANES], axis=0, keepdims=True)
+            jnp.sum(squares[p * outer : (p + 1) * outer], axis=0, keepdims=True)
             for p in range(probes)
         ]
-        hi = pixels.astype(BF16).astype(F32)
-        hi_lo = jnp.where(iota(pixels.shape, 1) < outer, hi, pixels - hi).astype(BF16)
-        return lines, outer_sums(hi_lo)
-
-    def outer_sums(hi_lo):
-        sums = dot(jnp.concatenate([hi_lo, hi_lo], axis=1), outer_ref[...])
-        return [sums[p * LANES : (p + 1) * LANES] for p in range(probes)]
+        hi, lo = halves(pixels)
+        sums = dot(jnp.concatenate([hi, lo, hi, lo], axis=1), inner_ref[...])
+        return lines, [sums[p * outer : (p + 1) * outer] for p in range(probes)]
 
     def finish_cycle(f, lines, sums):
         nonlocal power
         field = jnp.zeros((rows, count), F32)
         for p in range(probes):
             power = power + jnp.where(power_row == 2 * p, lines[p], 0.0)
-            cos_sum, sin_sum = twiddle_sums(sums[p], inner_cos, inner_sin)
+            cos_sum, sin_sum = twiddle_sums(sums[p], outer_ref[...])
             field = jnp.where(row == 2 * p, cos_sum, field)
             field = jnp.where(row == 2 * p + 1, sin_sum, field)
         for k in range(slots):
@@ -368,11 +368,11 @@
         mapped, done = later, (f, lines, sums)
     finish_cycle(*done)
     for f in range(cycles):
-        picked = mapped_ref[f, pl.ds(pl.multiple_of(own * LANES, LANES), LANES), :].T
-        weighted_ref[pl.ds(f, outer, stride=cycles), :] = picked[:outer] * fold(
-            signs_ref.at[0], f, 1
+        picked = mapped_ref[f, pl.ds(pl.multiple_of(own * outer, outer), outer), :]
+        weighted_ref[pl.ds(f, outer, stride=cycles), :] = picked * fold(
+            signs_ref.at[0], f
         ).astype(F32)
-    power = jnp.broadcast_to(0.5 * jnp.sum(power, axis=1, keepdims=True), (rows, per_slot))
+    power = jnp.broadcast_to(jnp.sum(power, axis=1, keepdims=True), (rows, per_slot))
     out = turned_rows(
         [pieces[k][f] for k in range(slots) for f in range(cycles)]
         + [scalars_ref[:, :per_slot], power]
@@ -397,10 +397,13 @@
     scalars = jnp.sum(by_core[0][start : start + 3 * rows], axis=1, keepdims=True)
     for values in by_core[1:]:
         scalars = scalars + jnp.sum(values[start : start + 3 * rows], axis=1, keepdims=True)
-    scalars = jnp.broadcast_to(scalars, (3 * rows, LANES))
+    lane = iota((rows, LANES), 1)
+    tile = jnp.where(
+        lane == 0, scalars[:rows], jnp.where(lane == 1, scalars[rows : 2 * rows], scalars[2 * rows :])
+    )
     for p in range(probes):
-        send_ref[p, 2 * block_rows : 2 * block_rows + 3 * rows, :] = scalars
-        send_ref[p, 2 * block_rows + 3 * rows :, :] = weighted_ref[...]
+        send_ref[p, 2 * block_rows : 2 * block_rows + rows, :] = tile
+        send_ref[p, 2 * block_rows + rows :, :] = weighted_ref[...]
     values = latitude_values(by_core, chosen_ref[...], slots, cycles, rows)
     first_degree = lax.axis_index("probe") * quarter
     signal = signal_ref[...]
@@ -428,17 +431,19 @@
     cycles, length = variance_ref.shape
     own = lax.axis_index("probe")
     start = 2 * block_rows
-    degree_sums = received_ref[0, start : start + 2 * rows, :]
-    for p in range(1, probes):
-        degree_sums = degree_sums + received_ref[p, start : start + 2 * rows, :]
-    norm, prior = degree_sums[:rows], degree_sums[rows:]
-    curve = prior + received_ref[0, start + 2 * rows : start + 3 * rows, :]
+    tiles = [received_ref[p, start : start + rows, :] for p in range(probes)]
+    degree_part = tiles[0]
+    for tile in tiles[1:]:
+        degree_part = degree_part + tile
+    shape = (rows, LANES)
+    norm = jnp.broadcast_to(degree_part[:, :1], shape)
+    curve = jnp.broadcast_to(degree_part[:, 1:2] + tiles[0][:, 2:3], shape)
     ratios = [
         (norm[2 * p : 2 * p + 1] + norm[2 * p + 1 : 2 * p + 2])
         / (curve[2 * p : 2 * p + 1] + curve[2 * p + 1 : 2 * p + 2])
         for p in range(probes)
     ]
-    start = start + 3 * rows
+    start = start + rows
     total = received_ref[0, start:, :] * ratios[0]
     for p in range(1, probes):
         total = total + received_ref[p, start:, :] * ratios[p]
@@ -487,7 +492,6 @@
     count = harmonic_order_values.shape[0]
     outer = length // LANES
     rows = probes * 2
-    by_order = ((LANES, count), F32)
     folded = ((outer * cycles, LANES), F32)
 
     def everywhere(send):
@@ -497,15 +501,14 @@
         return lax.all_gather(received, "core", axis=0)
 
     (
-        send, inner_cos, inner_sin, outer_table, limits, signs_near, row_line, signal,
+        send, inner_table, outer_table, limits, signs_near, row_line, signal,
         noise_near,
     ) = call(
         functools.partial(first_kernel, slots),
         [
             ((probes, places, LANES), F32),
-            by_order,
-            by_order,
-            ((4 * outer, 2 * count), BF16),
+            ((4 * LANES, 2 * count), BF16),
+            ((outer, 2 * count), F32),
             ((8, LANES), jnp.int32),
             (signs.shape, jnp.int32),
             ((1, total), jnp.int32),
@@ -543,12 +546,12 @@
     send, weighted = call(
         functools.partial(third_kernel, slots),
         [((places * cores, LANES), F32), folded],
-        [pltpu.VMEM((cycles, probes * LANES, LANES), F32)],
-        (received, signs_near, noise_near, inner_cos, inner_sin, outer_table, scalars),
+        [pltpu.VMEM((cycles, probes * outer, LANES), F32)],
+        (received, signs_near, noise_near, inner_table, outer_table, scalars),
         "cycles_there_and_back",
     )
     received = lax.all_to_all(send, ("place", "core"), 0, 0, tiled=True)
-    height = quarter // LANES * slots * 4 + 3 * rows + outer * cycles
+    height = quarter // LANES * slots * 4 + rows + outer * cycles
     (send,) = call(
         functools.partial(fourth_kernel, cores),
         [((probes, height, LANES), F32)],

time: 103 us -> 102 us (level)
  no operation moved by 1% of the time
where the time goes in v5:
time: 102 us
  blocking collectives  92.1 us (90%)
  Pallas kernels  8.97 us (9%)
    all_to_all x2, blocking collectives, everywhere(): lax.all_to_all(send.reshape(probes * places, LANES), ('probe', 'place'),...  55.7 us
    all_to_all x1, blocking collectives, per_device(): received = lax.all_to_all(send, ('place', 'core'), 0, 0, tiled=True)  16.6 us
    all_to_all x1, blocking collectives, per_device(): received = lax.all_to_all(send, 'probe', 0, 0, tiled=True)  12.5 us
    pallas_call x5, Pallas kernels, call(): pl.pallas_call(kernel, out_shape=[jax.ShapeDtypeStruct(shape, dtype) for...  8.97 us
    all_gather x2, blocking collectives, everywhere(): return lax.all_gather(received, 'core', axis=0)  7.33 us

profile of v5, /device:TPU:1, one launch (start us, length us, event | category | flops | bytes accessed | tf_op | source)
XLA Modules:
  0.0 101.7 jit_solution(3924496639383466266)
XLA Ops:
  0.6 0.0 copy-start
  0.6 2.0 %cycle_sums.1 = (f32[4,64,128]{2,1,0:T(8,128)S(1)}, bf16[512,512]{1,0:T(8,128)(2,1)S(1)}, f32[64,512]{1,0:T(8,128)S(1)}, s32[8,128]{1,0:T(8,128)S(1)}, s32[1,4,8...) custom-call(s32[1,256]{1,0:T(1,128)} %bitcast.23, ...), custom_call_target="tpu_custom_call" | custom-call | flops 2000000000 | bytes 20000000 | tf_op jit(solution)/shard_map/cycle_sums/pallas_call | solution.py:474
  2.6 34.9 %all_to_all.34 = f32[256,1,128]{2,1,0:T(1,128)S(1)} all-to-all(f32[256,1,128]{2,1,0:T(1,128)S(1)} %bitcast.17), channel_id=1, replica_groups=mesh['probe'=4,'place'=64,'core'=2] {'probe','place'}, dimensions={0} | all-to-all | bytes 262144 | tf_op jit(solution)/shard_map/all_to_all | solution.py:498
  37.5 3.9 %all-gather = f32[512,1,128]{2,1,0:T(1,128)S(1)} all-gather(f32[256,1,128]{2,1,0:T(1,128)S(1)} %all_to_all.34), channel_id=2, replica_groups=mesh['probe'=4,'place'=64,'core'=2] {'core'}, dimensions={0}, use_global_device_ids=true | all-gather | bytes 393216 | tf_op jit(solution)/shard_map/all_gather | solution.py:501
  41.4 0.0 copy-done
  41.4 2.7 %degrees_there_and_back.1 = (f32[4,64,128]{2,1,0:T(8,128)S(1)}, f32[2,8,1024]{2,1,0:T(8,128)S(1)}, f32[16,128]{1,0:T(8,128)S(1)}, bf16[2,1024,512]{2,1,0:T(8,128...) custom-call(f32[2,256,128]{2,1,0:T(8,128)S(1)} %bitcast.16, ...), custom_call_target="tpu_custom_call" | custom-call | flops 2000000000 | bytes 20000000 | tf_op jit(solution)/shard_map/degrees_there_and_back/pallas_call | solution.py:474
  44.0 20.8 %all_to_all.35 = f32[256,1,128]{2,1,0:T(1,128)S(1)} all-to-all(f32[256,1,128]{2,1,0:T(1,128)S(1)} %bitcast.18), channel_id=1, replica_groups=mesh['probe'=4,'place'=64,'core'=2] {'probe','place'}, dimensions={0} | all-to-all | bytes 262144 | tf_op jit(solution)/shard_map/all_to_all | solution.py:498
  64.8 3.5 %all-gather.1 = f32[512,1,128]{2,1,0:T(1,128)S(1)} all-gather(f32[256,1,128]{2,1,0:T(1,128)S(1)} %all_to_all.35), channel_id=3, replica_groups=mesh['probe'=4,'place'=64,'core'=2] {'core'}, dimensions={0}, use_global_device_ids=true | all-gather | bytes 393216 | tf_op jit(solution)/shard_map/all_gather | solution.py:501
  68.3 2.0 %cycles_there_and_back.1 = (f32[128,128]{1,0:T(8,128)S(1)}, f32[256,128]{1,0:T(8,128)S(1)}) custom-call(f32[2,256,128]{2,1,0:T(8,128)S(1)} %bitcast.15, s32[1,4,8192]{2,1,0:T(4,128)S(1)} %get-tuple-element.23.signs_ref, f32[4,8192]{1,0:T(4,128)S(1)} %get-tuple-element.24.inv_noise_ref, bf16[512,512]{1,0:T(8,128)(2,1)S(1)} %get-tuple-element.25.inner_ref, ...), custom_call_target="tpu_custom_call" | custom-call | flops 2000000000 | bytes 20000000 | tf_op jit(solution)/shard_map/cycles_there_and_back/pallas_call | solution.py:474
  70.3 16.6 %all_to_all.36 = f32[128,1,128]{2,1,0:T(1,128)S(1)} all-to-all(f32[128,1,128]{2,1,0:T(1,128)S(1)} %bitcast.20), channel_id=1, replica_groups=mesh['probe'=4,'place'=64,'core'=2] {'place','core'}, dimensions={0} | all-to-all | bytes 131072 | tf_op jit(solution)/shard_map/all_to_all | solution.py:553
  86.8 1.5 %image_terms.1 = f32[4,328,128]{2,1,0:T(8,128)S(1)} custom-call(f32[128,128]{1,0:T(8,128)S(1)} %bitcast.19, f32[1,1024]{1,0:T(1,128)S(1)} %get-tuple-element.20.signal_ref, s32[8,128]{1,0:T(8,128)S(1)} %get-tuple-element.21.limits_ref, bf16[2,1024,512]{2,1,0:T(8,128)(2,1)S(1)} %get-tuple-element.29.hi_ref, ...), custom_call_target="tpu_custom_call" | custom-call | flops 2000000000 | bytes 20000000 | tf_op jit(solution)/shard_map/image_terms/pallas_call | solution.py:474
  88.4 12.5 %all_to_all.37.received_ref = f32[4,328,128]{2,1,0:T(8,128)S(1)} all-to-all(f32[4,328,128]{2,1,0:T(8,128)S(1)} %image_terms.1), channel_id=1, replica_groups=mesh['probe'=4,'place'=64,'core'=2] {'probe'}, dimensions={0} | all-to-all | bytes 1343488 | tf_op jit(solution)/shard_map/all_to_all | solution.py:562
  100.9 0.9 outputs.1
Async XLA Ops:
  0.6 40.7 %copy-start = (f32[2,1024,512]{2,1,0:T(8,128)S(1)}, f32[2,1024,512]{2,1,0:T(8,128)}, u32[]{:S(2)}) copy-start(f32[2,1024,512]{2,1,0:T(8,128)} %legendre_ref.1) | copy-start | bytes 12582916

commit v6 on v5

--- a/solution.py
+++ b/solution.py
@@ -229,7 +229,7 @@
 
 def degree_sums(leg_hi, leg_lo, values, k, rows, order, first_degree):
     width = values.shape[0] // 2
-    across = dot_rows(values, leg_hi) + dot_rows(values, leg_lo)
+    across = dot(values, leg_hi) + dot(values, leg_lo)
     terms = across[k * rows : (k + 1) * rows] + across[
         width + k * rows : width + (k + 1) * rows
     ]
@@ -256,16 +256,12 @@
     signal = signal_ref[...]
     norm = jnp.zeros((rows, 1), F32)
     prior = jnp.zeros((rows, 1), F32)
-    halved = []
     for k in range(slots):
-        leg_hi, leg_lo = halves(legendre_ref[k])
-        hi_ref[k] = leg_hi
-        lo_ref[k] = leg_lo
-        halved.append((leg_hi, leg_lo))
+        hi_ref[k], lo_ref[k] = halves(legendre_ref[k].T)
     both = []
     for k in range(slots):
         terms = degree_sums(
-            *halved[k], values, k, rows, limits_ref[k : k + 1, :1], first_degree
+            hi_ref[k], lo_ref[k], values, k, rows, limits_ref[k : k + 1, :1], first_degree
         )
         terms_ref[k] = terms
         squares = terms * terms
@@ -274,7 +270,8 @@
         both.append(jnp.concatenate(halves(terms), axis=0))
     fields = []
     for k in range(slots):
-        field = dot(both[k], halved[k][0]) + dot(both[k], halved[k][1])
+        leg_hi, leg_lo = halves(legendre_ref[k])
+        field = dot(both[k], leg_hi) + dot(both[k], leg_lo)
         fields.append(field[:rows] + field[rows:])
     both = jnp.concatenate(halves(jnp.concatenate(fields, axis=0)), axis=0)
     by_cycle = dot(both, chosen)
@@ -386,7 +383,7 @@
     weighted_ref, send_ref,
 ):
     probes = send_ref.shape[0]
-    slots, quarter, total = hi_ref.shape
+    slots, total, quarter = hi_ref.shape
     cycles = total // received_ref.shape[0]
     places = received_ref.shape[0] // cores
     rows = probes * 2
@@ -534,8 +531,8 @@
             ((probes, places, LANES), F32),
             ((slots, rows, quarter), F32),
             ((2 * rows, LANES), F32),
-            (legendre.shape, BF16),
-            (legendre.shape, BF16),
+            ((slots, total, quarter), BF16),
+            ((slots, total, quarter), BF16),
             ((total, total), BF16),
         ],
         [],

time: 102 us -> 102 us (level)
  no operation moved by 1% of the time
where the time goes in v6:
time: 102 us; the launch traced here: 101 us
  blocking collectives  92.1 us (90%)
  Pallas kernels  8.53 us (8%)
    all_to_all x2, blocking collectives, everywhere(): lax.all_to_all(send.reshape(probes * places, LANES), ('probe', 'place'),...  55.7 us
    all_to_all x1, blocking collectives, per_device(): received = lax.all_to_all(send, ('place', 'core'), 0, 0, tiled=True)  16.6 us
    all_to_all x1, blocking collectives, per_device(): received = lax.all_to_all(send, 'probe', 0, 0, tiled=True)  12.5 us
    pallas_call x5, Pallas kernels, call(): pl.pallas_call(kernel, out_shape=[jax.ShapeDtypeStruct(shape, dtype) for...  8.53 us
    all_gather x2, blocking collectives, everywhere(): return lax.all_gather(received, 'core', axis=0)  7.33 us

profile of v6, /device:TPU:1, one launch (start us, length us, event | category | flops | bytes accessed | tf_op | source)
XLA Modules:
  0.0 101.3 jit_solution(13203139902423759317)
XLA Ops:
  0.6 0.0 copy-start
  0.6 2.0 %cycle_sums.1 = (f32[4,64,128]{2,1,0:T(8,128)S(1)}, bf16[512,512]{1,0:T(8,128)(2,1)S(1)}, f32[64,512]{1,0:T(8,128)S(1)}, s32[8,128]{1,0:T(8,128)S(1)}, s32[1,4,8...) custom-call(s32[1,256]{1,0:T(1,128)} %bitcast.23, ...), custom_call_target="tpu_custom_call" | custom-call | flops 2000000000 | bytes 20000000 | tf_op jit(solution)/shard_map/cycle_sums/pallas_call | solution.py:471
  2.6 34.9 %all_to_all.34 = f32[256,1,128]{2,1,0:T(1,128)S(1)} all-to-all(f32[256,1,128]{2,1,0:T(1,128)S(1)} %bitcast.17), channel_id=1, replica_groups=mesh['probe'=4,'place'=64,'core'=2] {'probe','place'}, dimensions={0} | all-to-all | bytes 262144 | tf_op jit(solution)/shard_map/all_to_all | solution.py:495
  37.5 3.9 %all-gather = f32[512,1,128]{2,1,0:T(1,128)S(1)} all-gather(f32[256,1,128]{2,1,0:T(1,128)S(1)} %all_to_all.34), channel_id=2, replica_groups=mesh['probe'=4,'place'=64,'core'=2] {'core'}, dimensions={0}, use_global_device_ids=true | all-gather | bytes 393216 | tf_op jit(solution)/shard_map/all_gather | solution.py:498
  41.4 0.0 copy-done
  41.4 2.7 %degrees_there_and_back.1 = (f32[4,64,128]{2,1,0:T(8,128)S(1)}, f32[2,8,1024]{2,1,0:T(8,128)S(1)}, f32[16,128]{1,0:T(8,128)S(1)}, bf16[2,512,1024]{2,1,0:T(8,128...) custom-call(f32[2,256,128]{2,1,0:T(8,128)S(1)} %bitcast.16, ...), custom_call_target="tpu_custom_call" | custom-call | flops 2000000000 | bytes 20000000 | tf_op jit(solution)/shard_map/degrees_there_and_back/pallas_call | solution.py:471
  44.0 20.8 %all_to_all.35 = f32[256,1,128]{2,1,0:T(1,128)S(1)} all-to-all(f32[256,1,128]{2,1,0:T(1,128)S(1)} %bitcast.18), channel_id=1, replica_groups=mesh['probe'=4,'place'=64,'core'=2] {'probe','place'}, dimensions={0} | all-to-all | bytes 262144 | tf_op jit(solution)/shard_map/all_to_all | solution.py:495
  64.8 3.5 %all-gather.1 = f32[512,1,128]{2,1,0:T(1,128)S(1)} all-gather(f32[256,1,128]{2,1,0:T(1,128)S(1)} %all_to_all.35), channel_id=3, replica_groups=mesh['probe'=4,'place'=64,'core'=2] {'core'}, dimensions={0}, use_global_device_ids=true | all-gather | bytes 393216 | tf_op jit(solution)/shard_map/all_gather | solution.py:498
  68.3 2.0 %cycles_there_and_back.1 = (f32[128,128]{1,0:T(8,128)S(1)}, f32[256,128]{1,0:T(8,128)S(1)}) custom-call(f32[2,256,128]{2,1,0:T(8,128)S(1)} %bitcast.15, s32[1,4,8192]{2,1,0:T(4,128)S(1)} %get-tuple-element.23.signs_ref, f32[4,8192]{1,0:T(4,128)S(1)} %get-tuple-element.24.inv_noise_ref, bf16[512,512]{1,0:T(8,128)(2,1)S(1)} %get-tuple-element.25.inner_ref, ...), custom_call_target="tpu_custom_call" | custom-call | flops 2000000000 | bytes 20000000 | tf_op jit(solution)/shard_map/cycles_there_and_back/pallas_call | solution.py:471
  70.3 16.6 %all_to_all.36 = f32[128,1,128]{2,1,0:T(1,128)S(1)} all-to-all(f32[128,1,128]{2,1,0:T(1,128)S(1)} %bitcast.20), channel_id=1, replica_groups=mesh['probe'=4,'place'=64,'core'=2] {'place','core'}, dimensions={0} | all-to-all | bytes 131072 | tf_op jit(solution)/shard_map/all_to_all | solution.py:550
  86.8 1.1 %image_terms.1 = f32[4,328,128]{2,1,0:T(8,128)S(1)} custom-call(f32[128,128]{1,0:T(8,128)S(1)} %bitcast.19, f32[1,1024]{1,0:T(1,128)S(1)} %get-tuple-element.20.signal_ref, s32[8,128]{1,0:T(8,128)S(1)} %get-tuple-element.21.limits_ref, bf16[2,512,1024]{2,1,0:T(8,128)(2,1)S(1)} %get-tuple-element.29.hi_ref, ...), custom_call_target="tpu_custom_call" | custom-call | flops 2000000000 | bytes 20000000 | tf_op jit(solution)/shard_map/image_terms/pallas_call | solution.py:471
  87.9 12.5 %all_to_all.37.received_ref = f32[4,328,128]{2,1,0:T(8,128)S(1)} all-to-all(f32[4,328,128]{2,1,0:T(8,128)S(1)} %image_terms.1), channel_id=1, replica_groups=mesh['probe'=4,'place'=64,'core'=2] {'probe'}, dimensions={0} | all-to-all | bytes 1343488 | tf_op jit(solution)/shard_map/all_to_all | solution.py:559
  100.4 0.9 outputs.1
Async XLA Ops:
  0.6 40.7 %copy-start = (f32[2,1024,512]{2,1,0:T(8,128)S(1)}, f32[2,1024,512]{2,1,0:T(8,128)}, u32[]{:S(2)}) copy-start(f32[2,1024,512]{2,1,0:T(8,128)} %legendre_ref.1) | copy-start | bytes 12582916

commit v7 on v6

--- a/solution.py
+++ b/solution.py
@@ -85,18 +85,18 @@
     return rows.T
 
 
-def own_rows(received_ref, source, groups):
-    places = received_ref.shape[1] // groups
-    total = received_ref[source, :places]
-    for g in range(1, groups):
-        total = total + received_ref[source, g * places : (g + 1) * places]
-    total = total.T
-    half = LANES // 2
-    return jnp.where(lax.axis_index("core") == 0, total[:half], total[half:])
+def device_of(place, tall, count):
+    return place % tall * (count // tall) + place // tall
+
+
+def store_by_device(rows, target_ref, tall):
+    lines = rows.shape[0] // tall
+    for n in range(lines):
+        target_ref[pl.ds(n, tall, stride=lines), :] = rows[n * tall : (n + 1) * tall]
 
 
 def first_kernel(
-    slots, orders_hbm, signs_hbm, rows_hbm, signal_hbm, noise_hbm,
+    slots, tall, orders_hbm, signs_hbm, rows_hbm, signal_hbm, noise_hbm,
     send_ref, inner_ref, outer_ref, limits_ref, signs_ref,
     rows_ref, signal_ref, noise_ref,
     orders_ref, near_rows_ref, sems,
@@ -105,7 +105,6 @@
     probes, places = send_ref.shape[:2]
     _, cycles, cycle_length = signs_ref.shape
     outer = cycle_length // LANES
-    cores = count // slots // places
     total = rows_ref.shape[1]
     own = lax.axis_index("probe")
     quarter = signal_ref.shape[1]
@@ -131,8 +130,7 @@
     outer_table = halves(cosine_and_sine(outer, cycle_length // outer, cycle_length))
     slot, place = iota((count, count), 0), iota((count, count), 1)
     slot_picks = ones_where(
-        slot == (place % places * cores + place // places % cores) * slots
-        + place // (places * cores)
+        slot == device_of(place % places, tall, places) * slots + place // places
     )
 
     copies[0].wait()
@@ -141,8 +139,9 @@
     parts = jnp.where(row == 0, orders >> 6, jnp.where(row == 1, orders & 63, 0))
     parts = dot(parts.astype(F32).astype(BF16), slot_picks).astype(jnp.int32)
     high, low = parts[:1], parts[1:2]
+    own_line = lax.axis_index("z") * lax.axis_size("core") + lax.axis_index("core")
     for k in range(slots):
-        own_place = (k * cores + lax.axis_index("core")) * places + lax.axis_index("place")
+        own_place = k * places + own_line * tall + lax.axis_index("y")
         picked = jnp.where(iota((1, count), 1) == own_place, high * 64 + low, 0).astype(F32)
         picked = jnp.sum(picked, axis=1, keepdims=True).astype(jnp.int32)
         limits_ref[k : k + 1, :] = jnp.broadcast_to(picked, (1, LANES))
@@ -176,16 +175,9 @@
         )
         for k in range(slots):
             pieces[k][f] = field[:, k * per_slot : (k + 1) * per_slot]
-    out = turned_rows(
-        [
-            pieces[k][f][:, c * places : (c + 1) * places]
-            for c in range(cores)
-            for k in range(slots)
-            for f in range(cycles)
-        ]
-    )
+    out = turned_rows([pieces[k][f] for k in range(slots) for f in range(cycles)])
     for p in range(probes):
-        send_ref[p] = out
+        store_by_device(out, send_ref.at[p], tall)
 
     for copy in copies[2:]:
         copy.wait()
@@ -194,8 +186,7 @@
     parts = jnp.where(row == 0, cycle_rows >> 6, jnp.where(row == 1, cycle_rows & 63, 0))
     cycle, place = iota((total, total), 0), iota((total, total), 1)
     picks = ones_where(
-        cycle == (place % places * cores + place // (places * cycles)) * cycles
-        + place // places % cycles
+        cycle == device_of(place % places, tall, places) * cycles + place // places
     )
     parts = dot(parts.astype(F32).astype(BF16), picks).astype(jnp.int32)
     rows_ref[...] = parts[:1] * 64 + parts[1:2]
@@ -211,12 +202,21 @@
     )
 
 
-def latitude_values(by_core, chosen, slots, cycles, rows):
+def join_kernel(tall, received_ref, out_ref):
+    places = out_ref.shape[0]
+    lines = places // tall
+    for n in range(lines):
+        total = received_ref[pl.ds(n, tall, stride=lines), :]
+        for start in range(places, received_ref.shape[0], places):
+            total = total + received_ref[pl.ds(start + n, tall, stride=lines), :]
+        out_ref[n * tall : (n + 1) * tall, :] = total
+
+
+def latitude_values(values, chosen, slots, cycles, rows):
     values = [
         jnp.concatenate(
             [
                 values[(k * cycles + f) * rows : (k * cycles + f + 1) * rows]
-                for values in by_core
                 for f in range(cycles)
             ],
             axis=1,
@@ -238,20 +238,17 @@
 
 
 def second_kernel(
-    received_ref, rows_ref, signal_ref, limits_ref, legendre_ref,
-    send_ref, terms_ref, scalars_ref, hi_ref, lo_ref, chosen_ref,
+    tall, received_ref, rows_ref, signal_ref, limits_ref, legendre_ref,
+    send_ref, terms_ref, hi_ref, lo_ref, chosen_ref,
 ):
-    cores = received_ref.shape[0]
     probes, places = send_ref.shape[:2]
     slots, quarter, total = legendre_ref.shape
-    cycles = total // (places * cores)
+    cycles = total // places
     rows = probes * 2
     width = slots * rows
     chosen = ones_where(iota((total, total), 0) == rows_ref[...])
     chosen_ref[...] = chosen
-    values = latitude_values(
-        [own_rows(received_ref, c, probes) for c in range(cores)], chosen, slots, cycles, rows
-    )
+    values = latitude_values(received_ref[...].T, chosen, slots, cycles, rows)
     first_degree = lax.axis_index("probe") * quarter
     signal = signal_ref[...]
     norm = jnp.zeros((rows, 1), F32)
@@ -278,31 +275,30 @@
     by_cycle = by_cycle[:width] + by_cycle[width:]
     out = turned_rows(
         [
-            by_cycle[k * rows : (k + 1) * rows, place * places : (place + 1) * places]
-            for c in range(cores)
+            by_cycle[k * rows : (k + 1) * rows, f * places : (f + 1) * places]
             for k in range(slots)
-            for place in range(c * cycles, (c + 1) * cycles)
+            for f in range(cycles)
         ]
+        + [jnp.broadcast_to(column, (rows, places)) for column in (norm, prior)]
     )
     for p in range(probes):
-        send_ref[p] = out
-    scalars_ref[:rows, :] = jnp.broadcast_to(norm, (rows, LANES))
-    scalars_ref[rows:, :] = jnp.broadcast_to(prior, (rows, LANES))
+        store_by_device(out, send_ref.at[p], tall)
 
 
 def third_kernel(
-    slots, received_ref, signs_ref, inv_noise_ref, inner_ref, outer_ref, scalars_ref,
-    send_ref, weighted_ref, mapped_ref,
+    slots, probes, tall, received_ref, signs_ref, inv_noise_ref, inner_ref, outer_ref,
+    send_ref, weighted_ref, scalars_ref, mapped_ref,
 ):
-    cores = received_ref.shape[0]
-    places = send_ref.shape[0] // cores
-    probes = received_ref.shape[1] // places
     cycles = inv_noise_ref.shape[0]
     outer, count = outer_ref.shape[0], outer_ref.shape[1] // 2
     rows = probes * 2
     own = lax.axis_index("probe")
 
-    by_core = [own_rows(received_ref, c, probes) for c in range(cores)]
+    received = received_ref[...].T
+    start = slots * cycles * rows
+    scalars_ref[...] = jnp.broadcast_to(
+        jnp.sum(received[start : start + 2 * rows], axis=1, keepdims=True), scalars_ref.shape
+    )
     outer_cos, outer_sin = outer_ref[:, :count], outer_ref[:, count:]
     per_slot = count // slots
     row = iota((rows, count), 0)
@@ -314,9 +310,8 @@
     def map_cycle(f):
         coeffs = jnp.concatenate(
             [
-                by_core[c][(k * cycles + f) * rows : (k * cycles + f + 1) * rows]
+                received[(k * cycles + f) * rows : (k * cycles + f + 1) * rows]
                 for k in range(slots)
-                for c in range(cores)
             ],
             axis=1,
         )
@@ -370,52 +365,59 @@
             signs_ref.at[0], f
         ).astype(F32)
     power = jnp.broadcast_to(jnp.sum(power, axis=1, keepdims=True), (rows, per_slot))
-    out = turned_rows(
-        [pieces[k][f] for k in range(slots) for f in range(cycles)]
-        + [scalars_ref[:, :per_slot], power]
-    )
-    for c in range(cores):
-        send_ref[pl.ds(c, places, stride=cores), :] = out[c * places : (c + 1) * places]
+    out = turned_rows([pieces[k][f] for k in range(slots) for f in range(cycles)] + [power])
+    store_by_device(out, send_ref, tall)
 
 
 def fourth_kernel(
-    cores, received_ref, signal_ref, limits_ref, hi_ref, lo_ref, chosen_ref, terms_ref,
-    weighted_ref, send_ref,
+    tall, received_ref, signal_ref, limits_ref, hi_ref, lo_ref, chosen_ref, terms_ref,
+    weighted_ref, scalars_ref, send_ref,
 ):
     probes = send_ref.shape[0]
     slots, total, quarter = hi_ref.shape
-    cycles = total // received_ref.shape[0]
-    places = received_ref.shape[0] // cores
+    places = received_ref.shape[0]
+    cycles = total // places
+    lines = places // tall
     rows = probes * 2
     blocks = quarter // LANES
     block_rows = blocks * slots * 2
-    by_core = [received_ref[pl.ds(c, places, stride=cores), :].T for c in range(cores)]
+    own = lax.axis_index("probe")
+    received = jnp.concatenate(
+        [received_ref[pl.ds(n, tall, stride=lines), :] for n in range(lines)], axis=0
+    ).T
+    values = latitude_values(received, chosen_ref[...], slots, cycles, rows)
     start = slots * cycles * rows
-    scalars = jnp.sum(by_core[0][start : start + 3 * rows], axis=1, keepdims=True)
-    for values in by_core[1:]:
-        scalars = scalars + jnp.sum(values[start : start + 3 * rows], axis=1, keepdims=True)
-    lane = iota((rows, LANES), 1)
-    tile = jnp.where(
-        lane == 0, scalars[:rows], jnp.where(lane == 1, scalars[rows : 2 * rows], scalars[2 * rows :])
-    )
+    norm = scalars_ref[:rows, :]
+    curve = scalars_ref[rows:, :] + jnp.sum(
+        received[start : start + rows], axis=1, keepdims=True
+    )
+    ratios = [
+        (norm[2 * p : 2 * p + 1] + norm[2 * p + 1 : 2 * p + 2])
+        / (curve[2 * p : 2 * p + 1] + curve[2 * p + 1 : 2 * p + 2])
+        for p in range(probes)
+    ]
+    own_ratio = ratios[0]
+    for p in range(1, probes):
+        own_ratio = jnp.where(own == p, ratios[p], own_ratio)
+    weighted = weighted_ref[...] * own_ratio
     for p in range(probes):
-        send_ref[p, 2 * block_rows : 2 * block_rows + rows, :] = tile
-        send_ref[p, 2 * block_rows + rows :, :] = weighted_ref[...]
-    values = latitude_values(by_core, chosen_ref[...], slots, cycles, rows)
-    first_degree = lax.axis_index("probe") * quarter
+        send_ref[p, block_rows:, :] = weighted
+    ratio = jnp.concatenate([ratios[p] for p in range(probes) for _ in range(2)], axis=0)
+    ratio = jnp.concatenate([ratio] * blocks, axis=1)
+    first_degree = own * quarter
     signal = signal_ref[...]
     for k in range(slots):
         noise_terms = degree_sums(
             hi_ref[k], lo_ref[k], values, k, rows, limits_ref[k : k + 1, :1], first_degree
         )
         terms = terms_ref[k]
-        image = signal * terms + noise_terms
+        residual = terms - ratio * (signal * terms + noise_terms)
         for p in range(probes):
             for b in range(blocks):
                 place = (b * slots + k) * 2
-                own = (slice(p * 2, p * 2 + 2), slice(b * LANES, (b + 1) * LANES))
-                send_ref[p, place : place + 2, :] = terms[own]
-                send_ref[p, block_rows + place : block_rows + place + 2, :] = image[own]
+                send_ref[p, place : place + 2, :] = residual[
+                    p * 2 : p * 2 + 2, b * LANES : (b + 1) * LANES
+                ]
 
 
 def last_kernel(received_ref, residual_ref, variance_ref):
@@ -423,43 +425,20 @@
     slots = residual_ref.shape[1]
     quarter = residual_ref.shape[3] // probes
     blocks = quarter // LANES
-    block_rows = blocks * slots * 2
-    rows = probes * 2
+    start = blocks * slots * 2
     cycles, length = variance_ref.shape
-    own = lax.axis_index("probe")
-    start = 2 * block_rows
-    tiles = [received_ref[p, start : start + rows, :] for p in range(probes)]
-    degree_part = tiles[0]
-    for tile in tiles[1:]:
-        degree_part = degree_part + tile
-    shape = (rows, LANES)
-    norm = jnp.broadcast_to(degree_part[:, :1], shape)
-    curve = jnp.broadcast_to(degree_part[:, 1:2] + tiles[0][:, 2:3], shape)
-    ratios = [
-        (norm[2 * p : 2 * p + 1] + norm[2 * p + 1 : 2 * p + 2])
-        / (curve[2 * p : 2 * p + 1] + curve[2 * p + 1 : 2 * p + 2])
-        for p in range(probes)
-    ]
-    start = start + rows
-    total = received_ref[0, start:, :] * ratios[0]
+    total = received_ref[0, start:, :]
     for p in range(1, probes):
-        total = total + received_ref[p, start:, :] * ratios[p]
+        total = total + received_ref[p, start:, :]
     total = total * (1.0 / probes)
     for j in range(length // LANES):
         variance_ref[:, j * LANES : (j + 1) * LANES] = total[j * cycles : (j + 1) * cycles]
-    own_ratio = ratios[0]
-    for p in range(1, probes):
-        own_ratio = jnp.where(own == p, ratios[p], own_ratio)
     for x in range(probes):
-        residual = (
-            received_ref[x, :block_rows, :]
-            - own_ratio * received_ref[x, block_rows : 2 * block_rows, :]
-        )
         for b in range(blocks):
             for k in range(slots):
                 place = x * quarter + b * LANES
                 row = (b * slots + k) * 2
-                residual_ref[0, k, :, place : place + LANES] = residual[row : row + 2]
+                residual_ref[0, k, :, place : place + LANES] = received_ref[x, row : row + 2, :]
 
 
 def call(kernel, outs, scratch, args, name, far=()):
@@ -484,24 +463,28 @@
     slots, quarter, total = legendre.shape
     _, cycles, length = signs.shape
     probes = lax.axis_size("probe")
-    places = lax.axis_size("place")
-    cores = lax.axis_size("core")
+    tall = lax.axis_size("y")
+    places = tall * lax.axis_size("z") * lax.axis_size("core")
     count = harmonic_order_values.shape[0]
     outer = length // LANES
     rows = probes * 2
     folded = ((outer * cycles, LANES), F32)
+    by_device = ((places, LANES), F32)
 
     def everywhere(send):
         received = lax.all_to_all(
-            send.reshape(probes * places, LANES), ("probe", "place"), 0, 0, tiled=True
-        )
-        return lax.all_gather(received, "core", axis=0)
+            send.reshape(probes * places, LANES), ("probe", "y"), 0, 0, tiled=True
+        )
+        (joined,) = call(
+            functools.partial(join_kernel, tall), [by_device], [], (received,), "join"
+        )
+        return lax.all_to_all(joined, ("z", "core"), 0, 0, tiled=True)
 
     (
         send, inner_table, outer_table, limits, signs_near, row_line, signal,
         noise_near,
     ) = call(
-        functools.partial(first_kernel, slots),
+        functools.partial(first_kernel, slots, tall),
         [
             ((probes, places, LANES), F32),
             ((4 * LANES, 2 * count), BF16),
@@ -525,12 +508,11 @@
         range(5),
     )
     received = everywhere(send)
-    send, terms, scalars, leg_hi, leg_lo, chosen = call(
-        second_kernel,
+    send, terms, leg_hi, leg_lo, chosen = call(
+        functools.partial(second_kernel, tall),
         [
             ((probes, places, LANES), F32),
             ((slots, rows, quarter), F32),
-            ((2 * rows, LANES), F32),
             ((slots, total, quarter), BF16),
             ((slots, total, quarter), BF16),
             ((total, total), BF16),
@@ -540,20 +522,20 @@
         "degrees_there_and_back",
     )
     received = everywhere(send)
-    send, weighted = call(
-        functools.partial(third_kernel, slots),
-        [((places * cores, LANES), F32), folded],
+    send, weighted, scalars = call(
+        functools.partial(third_kernel, slots, probes, tall),
+        [by_device, folded, ((2 * rows, LANES), F32)],
         [pltpu.VMEM((cycles, probes * outer, LANES), F32)],
-        (received, signs_near, noise_near, inner_table, outer_table, scalars),
+        (received, signs_near, noise_near, inner_table, outer_table),
         "cycles_there_and_back",
     )
-    received = lax.all_to_all(send, ("place", "core"), 0, 0, tiled=True)
-    height = quarter // LANES * slots * 4 + rows + outer * cycles
+    received = lax.all_to_all(send, ("y", "z", "core"), 0, 0, tiled=True)
+    height = quarter // LANES * slots * 2 + outer * cycles
     (send,) = call(
-        functools.partial(fourth_kernel, cores),
+        functools.partial(fourth_kernel, tall),
         [((probes, height, LANES), F32)],
         [],
-        (received, signal, limits, leg_hi, leg_lo, chosen, terms, weighted),
+        (received, signal, limits, leg_hi, leg_lo, chosen, terms, weighted, scalars),
         "image_terms",
     )
     received = lax.all_to_all(send, "probe", 0, 0, tiled=True)
@@ -568,10 +550,11 @@
 
 def solution(mesh):
     cores = 2
+    tall = math.isqrt(mesh.shape["sky"] // cores)
     split = jax.sharding.Mesh(
-        mesh.devices.reshape(mesh.shape["probe"], -1, cores), ("probe", "place", "core")
-    )
-    sky = ("place", "core")
+        mesh.devices.reshape(mesh.shape["probe"], tall, -1, cores), ("probe", "y", "z", "core")
+    )
+    sky = ("y", "z", "core")
     in_specs = (P(sky, "probe", None), P("probe", sky, None), P(sky, None), P(), P(), P())
     out_specs = (P("probe", sky, None, None), P(sky, None))
 

time: 102 us -> 107 us (1.049)
  blocking collectives: 92.1 us -> 98.1 us
    all_to_all x3 -> x5, blocking collectives: 72.3 us -> 86 us  [the longest x2 35.2 us: everywhere(): return lax.all_to_all(joined, ('z', 'core'), 0, 0, tiled=True)]
    all_gather x2 -> x0, blocking collectives: 7.33 us -> none  [everywhere(): return lax.all_gather(received, 'core', axis=0)]
    pallas_call x5 -> x7, Pallas kernels: 8.53 us -> 8.22 us  [call(): pl.pallas_call(kernel, out_shape=[jax.ShapeDtypeStruct(shape, dtype) for...]
where the time goes in v7:
time: 107 us
  blocking collectives  98.1 us (92%)
  Pallas kernels  8.22 us (8%)
    all_to_all x2, blocking collectives, everywhere(): return lax.all_to_all(joined, ('z', 'core'), 0, 0, tiled=True)  35.2 us
    all_to_all x2, blocking collectives, everywhere(): lax.all_to_all(send.reshape(probes * places, LANES), ('probe', 'y'), 0, 0...  34 us
    all_to_all x1, blocking collectives, per_device(): received = lax.all_to_all(send, ('y', 'z', 'core'), 0, 0, tiled=True)  16.9 us
    all_to_all x1, blocking collectives, per_device(): received = lax.all_to_all(send, 'probe', 0, 0, tiled=True)  12 us
    pallas_call x7, Pallas kernels, call(): pl.pallas_call(kernel, out_shape=[jax.ShapeDtypeStruct(shape, dtype) for...  8.22 us

profile of v7, /device:TPU:1, one launch (start us, length us, event | category | flops | bytes accessed | tf_op | source)
XLA Modules:
  0.0 107.0 jit_solution(1421555425775646715)
XLA Ops:
  0.6 1.8 %cycle_sums.1 = (f32[4,128,128]{2,1,0:T(8,128)S(1)}, bf16[512,512]{1,0:T(8,128)(2,1)S(1)}, f32[64,512]{1,0:T(8,128)S(1)}, s32[8,128]{1,0:T(8,128)S(1)}, s32[1,4,...) custom-call(s32[1,256]{1,0:T(1,128)} %bitcast.27, ...), custom_call_target="tpu_custom_call" | custom-call | flops 2000000000 | bytes 20000000 | tf_op jit(solution)/shard_map/cycle_sums/pallas_call | solution.py:450
  2.5 20.0 %all_to_all.60 = f32[32,16,128]{2,1,0:T(8,128)S(1)} all-to-all(f32[32,16,128]{2,1,0:T(8,128)S(1)} %bitcast.15), channel_id=1, replica_groups=mesh['probe'=4,'y'=8,'z'=8,'core'=2] {'probe','y'}, dimensions={0} | all-to-all | bytes 524288 | tf_op jit(solution)/shard_map/all_to_all | solution.py:475
  22.5 0.0 copy-start
  22.5 0.1 join.2
  22.6 21.9 %all_to_all.61 = f32[16,8,128]{2,1,0:T(8,128)S(1)} all-to-all(f32[16,8,128]{2,1,0:T(8,128)S(1)} %bitcast.23), channel_id=1, replica_groups=mesh['probe'=4,'y'=8,'z'=8,'core'=2] {'z','core'}, dimensions={0} | all-to-all | bytes 131072 | tf_op jit(solution)/shard_map/all_to_all | solution.py:481
  44.5 0.0 copy-done
  44.5 2.6 %degrees_there_and_back.1 = (f32[4,128,128]{2,1,0:T(8,128)S(1)}, f32[2,8,1024]{2,1,0:T(8,128)S(1)}, bf16[2,512,1024]{2,1,0:T(8,128)(2,1)S(1)}, bf16[2,512,1024]{2,1,0:T(8,128)(2,1)S(1)}, bf16[512,512]{1,0:T(8,128)(2,1)S(1)}) custom-call(f32[128,128]{1,0:T(8,128)S(1)} %bitcast.22, s32[1,512]{1,0:T(1,128)S(1)} %get-tuple-element.19.rows_ref, ...), custom_call_target="tpu_custom_call" | custom-call | flops 2000000000 | bytes 20000000 | tf_op jit(solution)/shard_map/degrees_there_and_back/pallas_call | solution.py:450
  47.1 14.0 %all_to_all.62 = f32[32,16,128]{2,1,0:T(8,128)S(1)} all-to-all(f32[32,16,128]{2,1,0:T(8,128)S(1)} %bitcast.16), channel_id=1, replica_groups=mesh['probe'=4,'y'=8,'z'=8,'core'=2] {'probe','y'}, dimensions={0} | all-to-all | bytes 524288 | tf_op jit(solution)/shard_map/all_to_all | solution.py:475
  61.1 0.1 join.3
  61.2 13.2 %all_to_all.63 = f32[16,8,128]{2,1,0:T(8,128)S(1)} all-to-all(f32[16,8,128]{2,1,0:T(8,128)S(1)} %bitcast.24), channel_id=1, replica_groups=mesh['probe'=4,'y'=8,'z'=8,'core'=2] {'z','core'}, dimensions={0} | all-to-all | bytes 131072 | tf_op jit(solution)/shard_map/all_to_all | solution.py:481
  74.5 1.9 %cycles_there_and_back.1 = (f32[128,128]{1,0:T(8,128)S(1)}, f32[256,128]{1,0:T(8,128)S(1)}, f32[16,128]{1,0:T(8,128)S(1)}) custom-call(f32[128,128]{1,0:T(8,128)S(1)} %bitcast.20, s32[1,4,8192]{2,1,0:T(4,128)S(1)} %get-tuple-element.23.signs_ref, f32[4,8192]{1,0:T(4,128)S(1)} %get-tuple-element.24.inv_noise_ref, ...), custom_call_target="tpu_custom_call" | custom-call | flops 2000000000 | bytes 20000000 | tf_op jit(solution)/shard_map/cycles_there_and_back/pallas_call | solution.py:450
  76.3 16.9 %all_to_all.64 = f32[128,1,128]{2,1,0:T(1,128)S(1)} all-to-all(f32[128,1,128]{2,1,0:T(1,128)S(1)} %bitcast.21), channel_id=1, replica_groups=mesh['probe'=4,'y'=8,'z'=8,'core'=2] {'y','z','core'}, dimensions={0} | all-to-all | bytes 131072 | tf_op jit(solution)/shard_map/all_to_all | solution.py:532
  93.2 1.0 image_terms.1
  94.3 12.0 %all_to_all.65.received_ref = f32[4,288,128]{2,1,0:T(8,128)S(1)} all-to-all(f32[4,288,128]{2,1,0:T(8,128)S(1)} %image_terms.1), channel_id=1, replica_groups=mesh['probe'=4,'y'=8,'z'=8,'core'=2] {'probe'}, dimensions={0} | all-to-all | bytes 1179648 | tf_op jit(solution)/shard_map/all_to_all | solution.py:541
  106.3 0.7 outputs.1
Async XLA Ops:
  22.5 22.0 %copy-start = (f32[2,1024,512]{2,1,0:T(8,128)S(1)}, f32[2,1024,512]{2,1,0:T(8,128)}, u32[]{:S(2)}) copy-start(f32[2,1024,512]{2,1,0:T(8,128)} %legendre_ref.1) | copy-start | bytes 12582916

commit v8 on v6

--- a/solution.py
+++ b/solution.py
@@ -256,8 +256,10 @@
     signal = signal_ref[...]
     norm = jnp.zeros((rows, 1), F32)
     prior = jnp.zeros((rows, 1), F32)
+    halved = []
     for k in range(slots):
-        hi_ref[k], lo_ref[k] = halves(legendre_ref[k].T)
+        halved.append(halves(legendre_ref[k]))
+        hi_ref[k], lo_ref[k] = halved[k][0].T, halved[k][1].T
     both = []
     for k in range(slots):
         terms = degree_sums(
@@ -270,8 +272,7 @@
         both.append(jnp.concatenate(halves(terms), axis=0))
     fields = []
     for k in range(slots):
-        leg_hi, leg_lo = halves(legendre_ref[k])
-        field = dot(both[k], leg_hi) + dot(both[k], leg_lo)
+        field = dot(both[k], halved[k][0]) + dot(both[k], halved[k][1])
         fields.append(field[:rows] + field[rows:])
     both = jnp.concatenate(halves(jnp.concatenate(fields, axis=0)), axis=0)
     by_cycle = dot(both, chosen)
@@ -309,7 +310,8 @@
     power = jnp.zeros((rows, LANES), F32)
     power_row = iota((rows, LANES), 0)
     pieces = [[None] * cycles for _ in range(slots)]
-    table = inner_ref[LANES : 3 * LANES, :]
+    table = inner_ref[LANES : 3 * LANES, :].T
+    table = jnp.concatenate([table, table], axis=0)
 
     def map_cycle(f):
         coeffs = jnp.concatenate(
@@ -328,8 +330,11 @@
             hi, lo = halves(jnp.concatenate([by_cos, by_sin], axis=1))
             high.append(hi)
             low.append(lo)
-        mapped = dot_rows(jnp.concatenate(high, axis=0), table) + dot_rows(
-            jnp.concatenate(low, axis=0), table
+        mapped = dot(
+            jnp.concatenate(
+                [jnp.concatenate(high, axis=0), jnp.concatenate(low, axis=0)], axis=1
+            ),
+            table,
         )
         return mapped[:, :LANES] + mapped[:, LANES:]
 

time: 102 us -> 101 us (level)
  no operation moved by 1% of the time
where the time goes in v8:
time: 101 us
  blocking collectives  92.1 us (91%)
  Pallas kernels  8.17 us (8%)
    all_to_all x2, blocking collectives, everywhere(): lax.all_to_all(send.reshape(probes * places, LANES), ('probe', 'place'),...  55.7 us
    all_to_all x1, blocking collectives, per_device(): received = lax.all_to_all(send, ('place', 'core'), 0, 0, tiled=True)  16.6 us
    all_to_all x1, blocking collectives, per_device(): received = lax.all_to_all(send, 'probe', 0, 0, tiled=True)  12.5 us
    pallas_call x5, Pallas kernels, call(): pl.pallas_call(kernel, out_shape=[jax.ShapeDtypeStruct(shape, dtype) for...  8.17 us
    all_gather x2, blocking collectives, everywhere(): return lax.all_gather(received, 'core', axis=0)  7.33 us

profile of v8, /device:TPU:1, one launch (start us, length us, event | category | flops | bytes accessed | tf_op | source)
XLA Modules:
  0.0 100.9 jit_solution(9436462411289302775)
XLA Ops:
  0.6 0.0 copy-start
  0.6 2.0 %cycle_sums.1 = (f32[4,64,128]{2,1,0:T(8,128)S(1)}, bf16[512,512]{1,0:T(8,128)(2,1)S(1)}, f32[64,512]{1,0:T(8,128)S(1)}, s32[8,128]{1,0:T(8,128)S(1)}, s32[1,4,8...) custom-call(s32[1,256]{1,0:T(1,128)} %bitcast.23, ...), custom_call_target="tpu_custom_call" | custom-call | flops 2000000000 | bytes 20000000 | tf_op jit(solution)/shard_map/cycle_sums/pallas_call | solution.py:476
  2.6 34.9 %all_to_all.34 = f32[256,1,128]{2,1,0:T(1,128)S(1)} all-to-all(f32[256,1,128]{2,1,0:T(1,128)S(1)} %bitcast.17), channel_id=1, replica_groups=mesh['probe'=4,'place'=64,'core'=2] {'probe','place'}, dimensions={0} | all-to-all | bytes 262144 | tf_op jit(solution)/shard_map/all_to_all | solution.py:500
  37.5 3.9 %all-gather = f32[512,1,128]{2,1,0:T(1,128)S(1)} all-gather(f32[256,1,128]{2,1,0:T(1,128)S(1)} %all_to_all.34), channel_id=2, replica_groups=mesh['probe'=4,'place'=64,'core'=2] {'core'}, dimensions={0}, use_global_device_ids=true | all-gather | bytes 393216 | tf_op jit(solution)/shard_map/all_gather | solution.py:503
  41.4 0.0 copy-done
  41.4 2.4 %degrees_there_and_back.1 = (f32[4,64,128]{2,1,0:T(8,128)S(1)}, f32[2,8,1024]{2,1,0:T(8,128)S(1)}, f32[16,128]{1,0:T(8,128)S(1)}, bf16[2,512,1024]{2,1,0:T(8,128...) custom-call(f32[2,256,128]{2,1,0:T(8,128)S(1)} %bitcast.16, ...), custom_call_target="tpu_custom_call" | custom-call | flops 2000000000 | bytes 20000000 | tf_op jit(solution)/shard_map/degrees_there_and_back/pallas_call | solution.py:476
  43.7 20.8 %all_to_all.35 = f32[256,1,128]{2,1,0:T(1,128)S(1)} all-to-all(f32[256,1,128]{2,1,0:T(1,128)S(1)} %bitcast.18), channel_id=1, replica_groups=mesh['probe'=4,'place'=64,'core'=2] {'probe','place'}, dimensions={0} | all-to-all | bytes 262144 | tf_op jit(solution)/shard_map/all_to_all | solution.py:500
  64.6 3.5 %all-gather.1 = f32[512,1,128]{2,1,0:T(1,128)S(1)} all-gather(f32[256,1,128]{2,1,0:T(1,128)S(1)} %all_to_all.35), channel_id=3, replica_groups=mesh['probe'=4,'place'=64,'core'=2] {'core'}, dimensions={0}, use_global_device_ids=true | all-gather | bytes 393216 | tf_op jit(solution)/shard_map/all_gather | solution.py:503
  68.0 1.9 %cycles_there_and_back.1 = (f32[128,128]{1,0:T(8,128)S(1)}, f32[256,128]{1,0:T(8,128)S(1)}) custom-call(f32[2,256,128]{2,1,0:T(8,128)S(1)} %bitcast.15, s32[1,4,8192]{2,1,0:T(4,128)S(1)} %get-tuple-element.23.signs_ref, f32[4,8192]{1,0:T(4,128)S(1)} %get-tuple-element.24.inv_noise_ref, bf16[512,512]{1,0:T(8,128)(2,1)S(1)} %get-tuple-element.25.inner_ref, ...), custom_call_target="tpu_custom_call" | custom-call | flops 2000000000 | bytes 20000000 | tf_op jit(solution)/shard_map/cycles_there_and_back/pallas_call | solution.py:476
  69.9 16.6 %all_to_all.36 = f32[128,1,128]{2,1,0:T(1,128)S(1)} all-to-all(f32[128,1,128]{2,1,0:T(1,128)S(1)} %bitcast.20), channel_id=1, replica_groups=mesh['probe'=4,'place'=64,'core'=2] {'place','core'}, dimensions={0} | all-to-all | bytes 131072 | tf_op jit(solution)/shard_map/all_to_all | solution.py:555
  86.5 1.1 %image_terms.1 = f32[4,328,128]{2,1,0:T(8,128)S(1)} custom-call(f32[128,128]{1,0:T(8,128)S(1)} %bitcast.19, f32[1,1024]{1,0:T(1,128)S(1)} %get-tuple-element.20.signal_ref, s32[8,128]{1,0:T(8,128)S(1)} %get-tuple-element.21.limits_ref, bf16[2,512,1024]{2,1,0:T(8,128)(2,1)S(1)} %get-tuple-element.29.hi_ref, ...), custom_call_target="tpu_custom_call" | custom-call | flops 2000000000 | bytes 20000000 | tf_op jit(solution)/shard_map/image_terms/pallas_call | solution.py:476
  87.6 12.5 %all_to_all.37.received_ref = f32[4,328,128]{2,1,0:T(8,128)S(1)} all-to-all(f32[4,328,128]{2,1,0:T(8,128)S(1)} %image_terms.1), channel_id=1, replica_groups=mesh['probe'=4,'place'=64,'core'=2] {'probe'}, dimensions={0} | all-to-all | bytes 1343488 | tf_op jit(solution)/shard_map/all_to_all | solution.py:564
  100.0 0.9 outputs.1
Async XLA Ops:
  0.6 40.7 %copy-start = (f32[2,1024,512]{2,1,0:T(8,128)S(1)}, f32[2,1024,512]{2,1,0:T(8,128)}, u32[]{:S(2)}) copy-start(f32[2,1024,512]{2,1,0:T(8,128)} %legendre_ref.1) | copy-start | bytes 12582916

commit v9 on v8

--- a/solution.py
+++ b/solution.py
@@ -399,10 +399,14 @@
     scalars = jnp.sum(by_core[0][start : start + 3 * rows], axis=1, keepdims=True)
     for values in by_core[1:]:
         scalars = scalars + jnp.sum(values[start : start + 3 * rows], axis=1, keepdims=True)
-    lane = iota((rows, LANES), 1)
-    tile = jnp.where(
-        lane == 0, scalars[:rows], jnp.where(lane == 1, scalars[rows : 2 * rows], scalars[2 * rows :])
-    )
+    norm = scalars[:rows]
+    curve = scalars[rows : 2 * rows] + scalars[2 * rows :] * (1.0 / probes)
+    pairs = [
+        part[2 * p : 2 * p + 1] + part[2 * p + 1 : 2 * p + 2]
+        for part in (norm, curve)
+        for p in range(probes)
+    ]
+    tile = jnp.broadcast_to(jnp.concatenate(pairs, axis=0), (rows, LANES))
     for p in range(probes):
         send_ref[p, 2 * block_rows : 2 * block_rows + rows, :] = tile
         send_ref[p, 2 * block_rows + rows :, :] = weighted_ref[...]
@@ -434,17 +438,10 @@
     own = lax.axis_index("probe")
     start = 2 * block_rows
     tiles = [received_ref[p, start : start + rows, :] for p in range(probes)]
-    degree_part = tiles[0]
+    sums = tiles[0]
     for tile in tiles[1:]:
-        degree_part = degree_part + tile
-    shape = (rows, LANES)
-    norm = jnp.broadcast_to(degree_part[:, :1], shape)
-    curve = jnp.broadcast_to(degree_part[:, 1:2] + tiles[0][:, 2:3], shape)
-    ratios = [
-        (norm[2 * p : 2 * p + 1] + norm[2 * p + 1 : 2 * p + 2])
-        / (curve[2 * p : 2 * p + 1] + curve[2 * p + 1 : 2 * p + 2])
-        for p in range(probes)
-    ]
+        sums = sums + tile
+    ratios = [sums[p : p + 1] / sums[probes + p : probes + p + 1] for p in range(probes)]
     start = start + rows
     total = received_ref[0, start:, :] * ratios[0]
     for p in range(1, probes):

time: 101 us -> 101 us (level)
  no operation moved by 1% of the time
where the time goes in v9:
time: 101 us
  blocking collectives  92.1 us (91%)
  Pallas kernels  8.03 us (8%)
    all_to_all x2, blocking collectives, everywhere(): lax.all_to_all(send.reshape(probes * places, LANES), ('probe', 'place'),...  55.7 us
    all_to_all x1, blocking collectives, per_device(): received = lax.all_to_all(send, ('place', 'core'), 0, 0, tiled=True)  16.6 us
    all_to_all x1, blocking collectives, per_device(): received = lax.all_to_all(send, 'probe', 0, 0, tiled=True)  12.5 us
    pallas_call x5, Pallas kernels, call(): pl.pallas_call(kernel, out_shape=[jax.ShapeDtypeStruct(shape, dtype) for...  8.03 us
    all_gather x2, blocking collectives, everywhere(): return lax.all_gather(received, 'core', axis=0)  7.33 us

profile of v9, /device:TPU:1, one launch (start us, length us, event | category | flops | bytes accessed | tf_op | source)
XLA Modules:
  0.0 100.8 jit_solution(5130063580682204903)
XLA Ops:
  0.6 0.0 copy-start
  0.6 2.0 %cycle_sums.1 = (f32[4,64,128]{2,1,0:T(8,128)S(1)}, bf16[512,512]{1,0:T(8,128)(2,1)S(1)}, f32[64,512]{1,0:T(8,128)S(1)}, s32[8,128]{1,0:T(8,128)S(1)}, s32[1,4,8...) custom-call(s32[1,256]{1,0:T(1,128)} %bitcast.23, ...), custom_call_target="tpu_custom_call" | custom-call | flops 2000000000 | bytes 20000000 | tf_op jit(solution)/shard_map/cycle_sums/pallas_call | solution.py:473
  2.6 34.9 %all_to_all.34 = f32[256,1,128]{2,1,0:T(1,128)S(1)} all-to-all(f32[256,1,128]{2,1,0:T(1,128)S(1)} %bitcast.17), channel_id=1, replica_groups=mesh['probe'=4,'place'=64,'core'=2] {'probe','place'}, dimensions={0} | all-to-all | bytes 262144 | tf_op jit(solution)/shard_map/all_to_all | solution.py:497
  37.5 3.9 %all-gather = f32[512,1,128]{2,1,0:T(1,128)S(1)} all-gather(f32[256,1,128]{2,1,0:T(1,128)S(1)} %all_to_all.34), channel_id=2, replica_groups=mesh['probe'=4,'place'=64,'core'=2] {'core'}, dimensions={0}, use_global_device_ids=true | all-gather | bytes 393216 | tf_op jit(solution)/shard_map/all_gather | solution.py:500
  41.4 0.0 copy-done
  41.4 2.4 %degrees_there_and_back.1 = (f32[4,64,128]{2,1,0:T(8,128)S(1)}, f32[2,8,1024]{2,1,0:T(8,128)S(1)}, f32[16,128]{1,0:T(8,128)S(1)}, bf16[2,512,1024]{2,1,0:T(8,128...) custom-call(f32[2,256,128]{2,1,0:T(8,128)S(1)} %bitcast.16, ...), custom_call_target="tpu_custom_call" | custom-call | flops 2000000000 | bytes 20000000 | tf_op jit(solution)/shard_map/degrees_there_and_back/pallas_call | solution.py:473
  43.7 20.8 %all_to_all.35 = f32[256,1,128]{2,1,0:T(1,128)S(1)} all-to-all(f32[256,1,128]{2,1,0:T(1,128)S(1)} %bitcast.18), channel_id=1, replica_groups=mesh['probe'=4,'place'=64,'core'=2] {'probe','place'}, dimensions={0} | all-to-all | bytes 262144 | tf_op jit(solution)/shard_map/all_to_all | solution.py:497
  64.6 3.5 %all-gather.1 = f32[512,1,128]{2,1,0:T(1,128)S(1)} all-gather(f32[256,1,128]{2,1,0:T(1,128)S(1)} %all_to_all.35), channel_id=3, replica_groups=mesh['probe'=4,'place'=64,'core'=2] {'core'}, dimensions={0}, use_global_device_ids=true | all-gather | bytes 393216 | tf_op jit(solution)/shard_map/all_gather | solution.py:500
  68.0 1.9 %cycles_there_and_back.1 = (f32[128,128]{1,0:T(8,128)S(1)}, f32[256,128]{1,0:T(8,128)S(1)}) custom-call(f32[2,256,128]{2,1,0:T(8,128)S(1)} %bitcast.15, s32[1,4,8192]{2,1,0:T(4,128)S(1)} %get-tuple-element.23.signs_ref, f32[4,8192]{1,0:T(4,128)S(1)} %get-tuple-element.24.inv_noise_ref, bf16[512,512]{1,0:T(8,128)(2,1)S(1)} %get-tuple-element.25.inner_ref, ...), custom_call_target="tpu_custom_call" | custom-call | flops 2000000000 | bytes 20000000 | tf_op jit(solution)/shard_map/cycles_there_and_back/pallas_call | solution.py:473
  69.9 16.6 %all_to_all.36 = f32[128,1,128]{2,1,0:T(1,128)S(1)} all-to-all(f32[128,1,128]{2,1,0:T(1,128)S(1)} %bitcast.20), channel_id=1, replica_groups=mesh['probe'=4,'place'=64,'core'=2] {'place','core'}, dimensions={0} | all-to-all | bytes 131072 | tf_op jit(solution)/shard_map/all_to_all | solution.py:552
  86.5 1.1 %image_terms.1 = f32[4,328,128]{2,1,0:T(8,128)S(1)} custom-call(f32[128,128]{1,0:T(8,128)S(1)} %bitcast.19, f32[1,1024]{1,0:T(1,128)S(1)} %get-tuple-element.20.signal_ref, s32[8,128]{1,0:T(8,128)S(1)} %get-tuple-element.21.limits_ref, bf16[2,512,1024]{2,1,0:T(8,128)(2,1)S(1)} %get-tuple-element.29.hi_ref, ...), custom_call_target="tpu_custom_call" | custom-call | flops 2000000000 | bytes 20000000 | tf_op jit(solution)/shard_map/image_terms/pallas_call | solution.py:473
  87.6 12.5 %all_to_all.37.received_ref = f32[4,328,128]{2,1,0:T(8,128)S(1)} all-to-all(f32[4,328,128]{2,1,0:T(8,128)S(1)} %image_terms.1), channel_id=1, replica_groups=mesh['probe'=4,'place'=64,'core'=2] {'probe'}, dimensions={0} | all-to-all | bytes 1343488 | tf_op jit(solution)/shard_map/all_to_all | solution.py:561
  100.0 0.7 outputs.1
Async XLA Ops:
  0.6 40.7 %copy-start = (f32[2,1024,512]{2,1,0:T(8,128)S(1)}, f32[2,1024,512]{2,1,0:T(8,128)}, u32[]{:S(2)}) copy-start(f32[2,1024,512]{2,1,0:T(8,128)} %legendre_ref.1) | copy-start | bytes 12582916
